TPU v7x, 512 devices: a whole 4x8x8 slice. The times are simulated.
512 devices in a mesh: dp: 256 (over z, y, x), ctx: 2 (over core).
Axes of the slice: x: 4, y: 8, z: 8, core: 2. Of those that a mesh axis runs over, the one named last changes fastest.
Arguments:
- head_inputs: float32 [512, 131072], P('ctx', 'dp'), may hold values from -30 to 30
- gate_inputs: float32 [512, 131072], P('ctx', 'dp'), may hold values from -6 to 6
- step_raw: float32 [2048, 512], P('dp', 'ctx'), may hold values from -4 to 4
- b_rows: float32 [16384, 512], P('dp', 'ctx'), may hold values from -6 to 6
- c_rows: float32 [16384, 512], P('dp', 'ctx'), may hold values from -0.125 to 0.125
- decay_log: float32 [2048], P('dp'), may hold values from -12 to -2
- step_bias: float32 [2048], P('dp'), may hold values from -1 to 1
- skip_gain: float32 [2048], P('dp'), may hold values from 0.5 to 1.5
- norm_gain: float32 [131072], P('dp'), may hold values from 0.1 to 1.9
- out_grad: float32 [512, 131072], P('ctx', 'dp'), may hold values from -16 to 16
Outputs:
- output: float32 [512, 131072], P('ctx', 'dp')
- head_grad: float32 [512, 131072], P('ctx', 'dp')
- gate_grad: float32 [512, 131072], P('ctx', 'dp')
- step_grad: float32 [2048, 512], P('dp', 'ctx')
- b_grad: float32 [16384, 512], P('dp', 'ctx')
- c_grad: float32 [16384, 512], P('dp', 'ctx')
- decay_grad: float32 [2048], P('dp')
- bias_grad: float32 [2048], P('dp')
- skip_grad: float32 [2048], P('dp')
- gain_grad: float32 [131072], P('dp')
All inputs are finite; a program needn't handle non-finite values.
Results may differ from a plain program's by a relative error of at most 0.0003.
Values sent between devices are 32-bit elements; how exact they have to be, the bound alone decides.
A program may use at most 64 MiB of HBM per device.

v0:
```python
import jax
import jax.numpy as jnp
from jax import lax
from jax.sharding import PartitionSpec as P

P_SIZE = 64
GROUP_DEVS = 4
Q = 128


HIGH = lax.Precision.HIGHEST
EPSILON = 1e-05


def from_partner(shard, axis, apart):
    return lax.ppermute(shard, axis, [(i, i ^ 1 << apart) for i in range(lax.axis_size(axis))])


def prefix(value, axis, join, neutral, backward):
    count, mine = (lax.axis_size(axis), lax.axis_index(axis))
    pieces = jax.tree.map(lambda part: lax.all_gather(part, axis), value)
    if backward:
        pieces = jax.tree.map(lambda part: part[::-1], pieces)
        mine = count - 1 - mine
    so_far = jax.tree.map(
        lambda part, zero: jnp.full_like(part, 0) + jnp.asarray(zero, part.dtype), value, neutral
    )

    def step(position, so_far):
        longer = join(so_far, jax.tree.map(lambda part: part[position], pieces))
        return jax.tree.map(lambda new, old: jnp.where(position < mine, new, old), longer, so_far)

    return lax.fori_loop(0, count - 1, step, so_far)


def stretch_scan(head_x, step_size, log_rate, b_group, c_group, state_init):
    length = head_x.shape[0]
    group_count = head_x.shape[1]
    per_group = head_x.shape[2]
    head_size = head_x.shape[3]
    blocks = length // Q
    x_blocks = head_x.reshape(blocks, Q, group_count, per_group, head_size)

    def to_blocks(array):
        return jnp.moveaxis(array.reshape(array.shape[:-1] + (blocks, Q)), -2, 0)

    positions = jnp.arange(Q)
    lower = positions[:, None] >= positions[None, :]

    def stretch_advance(state, block):
        x_part, step_part, rate_part, b_part, c_part = block
        running = jnp.cumsum(rate_part, axis=-1)
        gaps = running[..., :, None] - running[..., None, :]
        decay_mat = jnp.where(lower, jnp.exp(jnp.minimum(gaps, 0.0)), 0.0)
        scores = jnp.einsum("gni,gnj->gij", c_part, b_part, precision=HIGH)
        mixing = decay_mat * scores[:, None]
        scaled_x = x_part * jnp.transpose(step_part, (2, 0, 1))[..., None]
        inner = jnp.einsum("ghij,jghp->ighp", mixing, scaled_x, precision=HIGH)
        carried = jnp.einsum("gni,ghpn->ighp", c_part, state, precision=HIGH)
        carried = carried * jnp.transpose(jnp.exp(running), (2, 0, 1))[..., None]
        tail_decay = jnp.exp(running[..., -1:] - running)
        weighted_x = scaled_x * jnp.transpose(tail_decay, (2, 0, 1))[..., None]
        state_next = jnp.exp(running[..., -1])[..., None, None] * state
        state_next = state_next + jnp.einsum("gnj,jghp->ghpn", b_part, weighted_x, precision=HIGH)
        return (state_next, inner + carried)

    state_end, outputs = lax.scan(
        stretch_advance,
        state_init,
        (
            x_blocks,
            to_blocks(step_size),
            to_blocks(log_rate),
            to_blocks(b_group),
            to_blocks(c_group),
        ),
    )
    return (outputs.reshape(length, group_count, per_group, head_size), state_end)


def state_pass(head_x, step_size, log_rate, b_group):
    length = head_x.shape[0]
    blocks = length // Q
    x_blocks = head_x.reshape((blocks, Q) + head_x.shape[1:])

    def to_blocks(array):
        return jnp.moveaxis(array.reshape(array.shape[:-1] + (blocks, Q)), -2, 0)

    def state_advance(state, block):
        x_part, step_part, rate_part, b_part = block
        running = jnp.cumsum(rate_part, axis=-1)
        scaled_x = x_part * jnp.transpose(step_part, (2, 0, 1))[..., None]
        tail_decay = jnp.exp(running[..., -1:] - running)
        weighted_x = scaled_x * jnp.transpose(tail_decay, (2, 0, 1))[..., None]
        state_next = jnp.exp(running[..., -1])[..., None, None] * state
        state_next = state_next + jnp.einsum("gnj,jghp->ghpn", b_part, weighted_x, precision=HIGH)
        return (state_next, None)

    state_init = jnp.zeros(
        (head_x.shape[1], head_x.shape[2], head_x.shape[3], b_group.shape[1]), jnp.float32
    )
    state_end, unused_out = lax.scan(
        state_advance,
        state_init,
        (x_blocks, to_blocks(step_size), to_blocks(log_rate), to_blocks(b_group)),
    )
    return state_end


def chain_forward(earlier, later):
    return (earlier[0] * later[0], later[0][:, None, None] * earlier[1] + later[1])


def chain_backward(earlier, later):
    return (earlier[0] * later[0], later[1] + later[0][:, None, None] * earlier[1])


def group_total(values):
    result = values
    for bit_pos in range(GROUP_DEVS.bit_length() - 1):
        result = result + from_partner(result, "dp", bit_pos)
    return result


def group_total_back(values):
    result = values
    for bit_pos in range(GROUP_DEVS.bit_length() - 1):
        result = result + from_partner(result, "dp", bit_pos)
    return result


def shards(
    head_inputs,
    gate_inputs,
    step_raw,
    b_rows,
    c_rows,
    decay_log,
    step_bias,
    skip_gain,
    norm_gain,
    out_grad,
):
    length = head_inputs.shape[0]
    local_heads = decay_log.shape[0]
    group_width = local_heads * P_SIZE * GROUP_DEVS
    bit_count = GROUP_DEVS.bit_length() - 1
    dp_index = lax.axis_index("dp")
    stacked = jnp.stack((b_rows, c_rows))
    group_bc = stacked
    for bit_pos in range(bit_count):
        partner = from_partner(group_bc, "dp", bit_pos)
        upper = dp_index // (1 << bit_pos) % 2 == 1
        group_bc = jnp.where(
            upper, jnp.concatenate((partner, group_bc), 1), jnp.concatenate((group_bc, partner), 1)
        )
    b_group = group_bc[0]
    c_group = group_bc[1]
    step_size = jax.nn.softplus(step_raw + step_bias[:, None])
    log_rate = -jnp.exp(decay_log)[:, None] * step_size
    head_x = head_inputs.reshape(length, 1, local_heads, P_SIZE)
    local_state = state_pass(head_x, step_size[None], log_rate[None], b_group[None])[0]
    log_total = jnp.sum(log_rate, axis=1)
    decay_total = jnp.exp(log_total)
    carried = prefix(
        (decay_total, local_state),
        "ctx",
        chain_forward,
        (jnp.ones_like(decay_total), jnp.zeros_like(local_state)),
        False,
    )
    state_init = carried[1]

    def local_forward(head_part, raw_part, bias_part, rate_part, b_part, c_part, state_part):
        size_part = jax.nn.softplus(raw_part + bias_part[:, None])
        logs_part = -jnp.exp(rate_part)[:, None] * size_part
        mixed_part, state_end = stretch_scan(
            head_part.reshape(length, 1, local_heads, P_SIZE),
            size_part[None],
            logs_part[None],
            b_part[None],
            c_part[None],
            state_part[None],
        )
        return (mixed_part.reshape(length, local_heads * P_SIZE), state_end[0])

    primal, pullback = jax.vjp(
        local_forward, head_inputs, step_raw, step_bias, decay_log, b_group, c_group, state_init
    )
    skip_row = jnp.repeat(skip_gain, P_SIZE)
    mixed = primal[0] + skip_row * head_inputs
    gate_value = jax.nn.silu(gate_inputs)
    gated = mixed * gate_value
    total_squares = group_total(jnp.sum(gated * gated, axis=1))
    inverse = lax.rsqrt(total_squares / group_width + EPSILON)
    normed = gated * inverse[:, None]
    output = normed * norm_gain
    scaled_grad = out_grad * norm_gain
    gain_local = jnp.sum(out_grad * normed, axis=0)
    cross = group_total_back(jnp.sum(scaled_grad * gated, axis=1))
    gated_grad = (
        scaled_grad * inverse[:, None]
        - gated * (inverse * inverse * inverse * cross / group_width)[:, None]
    )
    sigmoid_z = jax.nn.sigmoid(gate_inputs)
    gate_grad = gated_grad * mixed * sigmoid_z * (1.0 + gate_inputs * (1.0 - sigmoid_z))
    mixed_grad = gated_grad * gate_value
    skip_local = jnp.sum(
        (mixed_grad * head_inputs).reshape(length, local_heads, P_SIZE), axis=(0, 2)
    )
    weighted = (
        mixed_grad.reshape(length, local_heads, P_SIZE)
        * jnp.exp(jnp.cumsum(log_rate, axis=1)).T[:, :, None]
    )
    start_grad = jnp.einsum("thp,nt->hpn", weighted, c_group, precision=HIGH)
    carried_grad = prefix(
        (decay_total, start_grad),
        "ctx",
        chain_backward,
        (jnp.ones_like(decay_total), jnp.zeros_like(start_grad)),
        True,
    )
    end_grad = carried_grad[1]
    grads = pullback((mixed_grad, end_grad))
    head_grad = grads[0] + mixed_grad * skip_row
    bc_mine = jnp.stack((grads[4], grads[5]))
    for step_back in range(bit_count):
        bit_pos = bit_count - 1 - step_back
        half = bc_mine.shape[1] // 2
        lower_half = bc_mine[:, :half]
        upper_half = bc_mine[:, half:]
        upper = dp_index // (1 << bit_pos) % 2 == 1
        keep_half = jnp.where(upper, upper_half, lower_half)
        send_half = jnp.where(upper, lower_half, upper_half)
        bc_mine = keep_half + from_partner(send_half, "dp", bit_pos)
    sums = lax.psum((grads[3], grads[2], skip_local, gain_local), "ctx")
    return (
        output,
        head_grad,
        gate_grad,
        grads[1],
        bc_mine[0],
        bc_mine[1],
        sums[0],
        sums[1],
        sums[2],
        sums[3],
    )


def solution(mesh):
    in_specs = (
        P("ctx", "dp"),
        P("ctx", "dp"),
        P("dp", "ctx"),
        P("dp", "ctx"),
        P("dp", "ctx"),
        P("dp"),
        P("dp"),
        P("dp"),
        P("dp"),
        P("ctx", "dp"),
    )
    out_specs = (
        P("ctx", "dp"),
        P("ctx", "dp"),
        P("ctx", "dp"),
        P("dp", "ctx"),
        P("dp", "ctx"),
        P("dp", "ctx"),
        P("dp"),
        P("dp"),
        P("dp"),
        P("dp"),
    )
    return jax.shard_map(shards, mesh=mesh, in_specs=in_specs, out_specs=out_specs, check_vma=False)
```

profile of v0, /device:TPU:1, one launch (start us, length us, event | category | flops | bytes accessed | tf_op | source)
XLA Modules:
  0.0 232.2 jit_solution(8580654040096861284)
XLA Ops:
  8.2 3.9 %collective-permute-start = (f32[2,64,256]{2,1,0:T(8,128)S(1)}, f32[2,64,256]{2,1,0:T(8,128)S(1)}, u32[]{:S(2)}, u32[]{:S(2)}) collective-permute-start(f32[2,64,256]{2,1,0:T(8,128)S(1)} %pad_maximum_fusion.1), channel_id=1, source_target_pairs={{0,2},{2,0},{4,6},{6,4},{8,10},{10,8},{12,14},{14,12},{16,18},{18,... | collective-permute-start | bytes 393224 | tf_op jit(solution)/shard_map/ppermute | solution.py:16
  12.1 2.3 collective-permute-done
  15.4 5.4 %collective-permute-start.1 = (f32[2,128,256]{2,1,0:T(8,128)S(1)}, f32[2,128,256]{2,1,0:T(8,128)S(1)}, u32[]{:S(2)}, u32[]{:S(2)}) collective-permute-start(f32[2,128,256]{2,1,0:T(8,128)S(1)} %maximum_select_fusion.1), channel_id=1, source_target_pairs={{0,4},{2,6},{4,0},{6,2},{8,12},{10,14},{12,8},{14,10},{16,20},{18,... | collective-permute-start | bytes 786440 | tf_op jit(solution)/shard_map/ppermute | solution.py:16
  25.5 2.9 %while.95 = (s32[]{:T(128)}, f32[1,8,64,256]{3,2,1,0:T(8,128)S(1)}, f32[2,1,8,128]{3,2,1,0:T(8,128)S(1)}, f32[2,128,1,8,64]{1,4,3,2,0:T(8,128)S(1)}, f32[2,1,8,1...) while((s32[]{:T(128)}, f32[1,8,64,256]{3,2,1,0:T(8,128)S(1)}, ...), condition=%wide.region_3.4_spmd.clone, body=%wide.region_1.3_spmd.clone.sunk | while | flops 201981952 | bytes 1484563 | solution.py:102
  31.8 1.3 dynamic-slice
  33.8 10.1 %all-reduce.2 = f32[16]{0:T(128)S(1)} all-reduce(f32[16]{0:T(128)S(1)} %exponential_dynamic-update-slice_fusion), channel_id=2, replica_groups=mesh['dp'=256,'ctx'=2] {'ctx'}, use_global_device_ids=true, to_apply=%add.2 | all-reduce | flops 16 | bytes 128
  44.5 11.1 %all-gather.5.cloned.1.call-done = f32[2,8,64,256]{3,2,1,0:T(8,128)} async-done(((f32[1,8,64,256]{3,2,1,0:T(8,128)}), f32[2,8,64,256]{3,2,1,0:T(8,128)}) %all-gather.5.cloned.1.call-update) | async-done | bytes 1048592 | tf_op jit(solution)/shard_map/all_gather | solution.py:21
  57.8 36.3 %while.94 = (s32[]{:T(128)}, f32[1,8,64,256]{3,2,1,0:T(8,128)S(1)}, f32[2,128,1,8,64]{1,0,4,3,2:T(2,128)}, f32[2,1,8,128,128]{4,3,2,1,0:T(8,128)}, f32[2,1,8,128...) while((s32[]{:T(128)}, f32[1,8,64,256]{3,2,1,0:T(8,128)S(1)}, ...), condition=%wide.region_6.7_spmd.clone.clone, body=%wide.region_4.6_spmd.clone.clone.sunk | while | flops 556075008 | bytes 16996184 | solution.py:67
  59.9 1.3 bitcast_dynamic-update-slice_fusion.6
  61.1 1.2 fusion.218
  62.3 7.2 %dynamic_update_slice.225 = f32[2,128,1,8,64]{1,0,4,3,2:T(2,128)} dynamic-update-slice(f32[2,128,1,8,64]{1,0,4,3,2:T(2,128)} %get-tuple-element.1937, f32[1,128,1,8,64]{1,0,4,3,2:T(1,128)S(1)} %bitcast.570, s32[]{:T(128)} %get-tuple-element.1935, s32[]{:T(128)} %constant.238.clone.1..sunk.1, s32[]{:T(128)} %constant.238.clone.1..sunk.1, s32[]{:T(128)} %constant.238.clone.1..sunk.1, ...) | dynamic-update-slice | bytes 524292 | tf_op jit(solution)/shard_map/jvp()/while/body/jit(dynamic_update_index_in_dim)/dynamic_update_slice | solution.py:67
  71.5 1.5 fusion.219
  78.0 1.3 bitcast_dynamic-update-slice_fusion.6
  79.3 1.2 fusion.218
  80.5 7.2 %dynamic_update_slice.225 = f32[2,128,1,8,64]{1,0,4,3,2:T(2,128)} dynamic-update-slice(f32[2,128,1,8,64]{1,0,4,3,2:T(2,128)} %get-tuple-element.1937, f32[1,128,1,8,64]{1,0,4,3,2:T(1,128)S(1)} %bitcast.570, s32[]{:T(128)} %get-tuple-element.1935, s32[]{:T(128)} %constant.238.clone.1..sunk.1, s32[]{:T(128)} %constant.238.clone.1..sunk.1, s32[]{:T(128)} %constant.238.clone.1..sunk.1, ...) | dynamic-update-slice | bytes 524292 | tf_op jit(solution)/shard_map/jvp()/while/body/jit(dynamic_update_index_in_dim)/dynamic_update_slice | solution.py:67
  89.7 1.5 fusion.219
  94.8 2.4 %multiply_reduce_fusion.3 = (f32[256]{0:T(256)S(1)}, f32[256,512]{0,1:T(8,128)}) fusion(f32[256,512]{0,1:T(8,128)} %copy.98, f32[256,512]{0,1:T(8,128)} %copy-done.3, f32[512]{0:T(512)S(1)} %copy-done.25, f32[64,8,2,128]{3,2,1,0:T(2,128)} %bitcast.573), kind=kLoop, calls=%fused_computation.192 | loop fusion | flops 1179392 | bytes 2100224 | tf_op jit(solution)/shard_map/reduce_sum | solution.py:194
  97.2 2.1 collective-permute-start.2
  99.3 2.2 collective-permute-done.2
  101.5 3.7 %collective-permute-start.3 = (f32[256]{0:T(256)S(1)}, f32[256]{0:T(256)S(1)}, u32[]{:S(2)}, u32[]{:S(2)}) collective-permute-start(f32[256]{0:T(256)S(1)} %add.148), channel_id=1, source_target_pairs={{0,4},{2,6},{4,0},{6,2},{8,12},{10,14},{12,8},{14,10},{16,20},{18,... | collective-permute-start | bytes 3080 | tf_op jit(solution)/shard_map/ppermute | solution.py:16
  107.5 2.1 multiply_reduce_fusion
  109.6 2.2 collective-permute-start.4
  112.0 1.9 collective-permute-done.4
  113.9 3.7 %collective-permute-start.5 = (f32[256]{0:T(256)S(1)}, f32[256]{0:T(256)S(1)}, u32[]{:S(2)}, u32[]{:S(2)}) collective-permute-start(f32[256]{0:T(256)S(1)} %add.152), channel_id=1, source_target_pairs={{0,4},{2,6},{4,0},{6,2},{8,12},{10,14},{12,8},{14,10},{16,20},{18,... | collective-permute-start | bytes 3080 | tf_op jit(solution)/shard_map/ppermute | solution.py:16
  117.7 2.0 collective-permute-done.5
  119.7 2.9 %multiply_reduce_fusion.1 = (f32[512]{0:T(512)S(1)}, f32[256,512]{0,1:T(8,128)S(1)}, f32[256,512]{0,1:T(8,128)}, f32[256,512]{0,1:T(8,128)}) fusion(f32[256,512]{0,1:T(8,128)S(1)} %copy-done.4, f32[256,512]{0,1:T(8,128)} %copy.98, f32[256,512]{0,1:T(8,128)} %get-tuple-element.1426, f32[256]{0:T(256)S(1)} %fusion.133, f32[256]{0:T(256)S(1)} %add_rsqrt_fusion, ...), kind=kLoop, calls=%fused_computation.188 | loop fusion | flops 2752000 | bytes 4202496 | tf_op jit(solution)/shard_map/reduce_sum | solution.py:208
  123.8 1.4 fusion.123
  127.4 2.1 copy.108
  130.6 17.8 %all-gather.7.cloned.1.call-done = f32[16,64,256]{2,1,0:T(8,128)} async-done(((f32[8,64,256]{2,1,0:T(8,128)}), f32[16,64,256]{2,1,0:T(8,128)}) %all-gather.7.cloned.1.call-update) | async-done | bytes 1048592 | tf_op jit(solution)/shard_map/all_gather | solution.py:21
  152.7 51.4 %while.93 = (s32[]{:T(128)}, f32[1,8,64,256]{3,2,1,0:T(8,128)S(1)}, f32[2,128,1,8,64]{1,0,4,3,2:T(2,128)}, f32[2,1,8,128]{3,2,1,0:T(8,128)S(1)}, f32[2,1,8,128]{...) while((s32[]{:T(128)}, f32[1,8,64,256]{3,2,1,0:T(8,128)S(1)}, ...), condition=%wide.region_21.22_spmd.clone, body=%wide.region_11.21_spmd.clone.sunk | while | flops 1109775360 | bytes 21576568 | solution.py:67
  152.7 1.5 constant_dynamic-slice_fusion.11
  155.1 2.4 %fusion.204 = (f32[128,128]{1,0:T(8,128)S(1)}, f32[8,128,128]{2,1,0:T(8,128)S(1)}) fusion(f32[2,1,8,128,128]{4,3,2,1,0:T(8,128)} %get-tuple-element.2079, s32[]{:T(128)S(6)} %sub.240, f32[2,1,8,128,128]{4,3,2,1,0:T(8,128)} %get-tuple-element.2077, f32[2,1,8,128,128]{4,3,2,1,0:T(8,128)} %get-tuple-element.2076, ...), kind=kOutput, calls=%fused_computation.18.clone.1 | convolution fusion | flops 101433344 | bytes 2769920 | tf_op jit(solution)/shard_map/transpose(jvp())/while/body/eval_jaxpr/ghij,jghp->ighp/dot_general | solution.py:58
  157.7 1.5 fusion.200
  161.5 1.2 reduce_window_sum.60
  162.8 1.6 fusion.202
  167.0 7.1 %dynamic_update_slice.215 = f32[2,128,1,8,64]{1,0,4,3,2:T(2,128)} dynamic-update-slice(f32[2,128,1,8,64]{1,0,4,3,2:T(2,128)} %get-tuple-element.2024, f32[1,128,1,8,64]{1,0,4,3,2:T(1,128)S(1)} %bitcast.569, s32[]{:T(128)S(6)} %sub.240, s32[]{:T(128)} %constant.238.clone.1..sunk, s32[]{:T(128)} %constant.238.clone.1..sunk, s32[]{:T(128)} %constant.238.clone.1..sunk, s32[]{:T(128)} %constant.238.clone.1..sunk) | dynamic-update-slice | bytes 524292 | tf_op jit(solution)/shard_map/transpose(jvp())/while/body/jit(dynamic_update_index_in_dim)/dynamic_update_slice | solution.py:67
  175.1 1.6 fusion.210
  178.4 1.5 constant_dynamic-slice_fusion.11
  180.8 2.4 %fusion.204 = (f32[128,128]{1,0:T(8,128)S(1)}, f32[8,128,128]{2,1,0:T(8,128)S(1)}) fusion(f32[2,1,8,128,128]{4,3,2,1,0:T(8,128)} %get-tuple-element.2079, s32[]{:T(128)S(6)} %sub.240, f32[2,1,8,128,128]{4,3,2,1,0:T(8,128)} %get-tuple-element.2077, f32[2,1,8,128,128]{4,3,2,1,0:T(8,128)} %get-tuple-element.2076, ...), kind=kOutput, calls=%fused_computation.18.clone.1 | convolution fusion | flops 101433344 | bytes 2769920 | tf_op jit(solution)/shard_map/transpose(jvp())/while/body/eval_jaxpr/ghij,jghp->ighp/dot_general | solution.py:58
  183.4 1.5 fusion.200
  187.2 1.2 reduce_window_sum.60
  188.5 1.6 fusion.202
  192.7 7.1 %dynamic_update_slice.215 = f32[2,128,1,8,64]{1,0,4,3,2:T(2,128)} dynamic-update-slice(f32[2,128,1,8,64]{1,0,4,3,2:T(2,128)} %get-tuple-element.2024, f32[1,128,1,8,64]{1,0,4,3,2:T(1,128)S(1)} %bitcast.569, s32[]{:T(128)S(6)} %sub.240, s32[]{:T(128)} %constant.238.clone.1..sunk, s32[]{:T(128)} %constant.238.clone.1..sunk, s32[]{:T(128)} %constant.238.clone.1..sunk, s32[]{:T(128)} %constant.238.clone.1..sunk) | dynamic-update-slice | bytes 524292 | tf_op jit(solution)/shard_map/transpose(jvp())/while/body/jit(dynamic_update_index_in_dim)/dynamic_update_slice | solution.py:67
  200.8 1.6 fusion.210
  205.5 3.7 %collective-permute-start.6 = (f32[2,128,256]{2,1,0:T(8,128)S(1)}, f32[2,128,256]{2,1,0:T(8,128)S(1)}, u32[]{:S(2)}, u32[]{:S(2)}) collective-permute-start(f32[2,128,256]{2,1,0:T(8,128)S(1)} %broadcast_select_fusion), channel_id=1, source_target_pairs={{0,4},{2,6},{4,0},{6,2},{8,12},{10,14},{12,8},{14,10},{16,20},{18,... | collective-permute-start | bytes 786440 | tf_op jit(solution)/shard_map/ppermute | solution.py:16
  210.9 5.8 %collective-permute-done.6 = f32[2,128,256]{2,1,0:T(8,128)S(1)} collective-permute-done((f32[2,128,256]{2,1,0:T(8,128)S(1)}, f32[2,128,256]{2,1,0:T(8,128)S(1)}, u32[]{:S(2)}, u32[]{:S(2)}) %collective-permute-start.6) | collective-permute-done | bytes 262176 | tf_op jit(solution)/shard_map/ppermute | solution.py:16
  216.9 2.1 collective-permute-start.7
  219.7 4.0 %all-reduce.3 = (f32[8]{0:T(128)}, f32[8]{0:T(128)}, f32[8]{0:T(128)}, f32[512]{0:T(512)}) all-reduce(f32[8]{0:T(128)S(1)} %negate_multiply_fusion, f32[8]{0:T(128)S(1)} %get-tuple-element.1423, f32[8]{0:T(128)S(1)} %reduce_sum.184, f32[512]{0:T(512)S(1)} %copy-done.34), channel_id=1, replica_groups=mesh['dp'=256,'ctx'=2] {'ctx'}, use_global_device_ids=true, to_apply=%region_23.24 | all-reduce | flops 536 | bytes 4288 | tf_op jit(solution)/shard_map/psum | solution.py:236
  (290 shorter events, 63.8 us)
Async XLA Ops:
  7.2 13.8 %copy-start.19 = (f32[256,512]{1,0:T(8,128)S(1)}, f32[256,512]{1,0:T(8,128)}, u32[]{:S(2)}) copy-start(f32[256,512]{1,0:T(8,128)} %param.16) | copy-start | bytes 1572868
  7.2 48.5 %all-gather.5.cloned.1.call-start = ((), (), s32[]{:S(2)}) async-start(), calls=%async_computation | async-start | bytes 1572864 | tf_op jit(solution)/shard_map/all_gather | solution.py:21
  8.2 6.3 %collective-permute-start = (f32[2,64,256]{2,1,0:T(8,128)S(1)}, f32[2,64,256]{2,1,0:T(8,128)S(1)}, u32[]{:S(2)}, u32[]{:S(2)}) collective-permute-start(f32[2,64,256]{2,1,0:T(8,128)S(1)} %pad_maximum_fusion.1), channel_id=1, source_target_pairs={{0,2},{2,0},{4,6},{6,4},{8,10},{10,8},{12,14},{14,12},{16,18},{18,... | collective-permute-start | bytes 393224 | tf_op jit(solution)/shard_map/ppermute | solution.py:16
  12.1 8.7 %copy-start.41 = (f32[8]{0:T(128)S(1)}, f32[8]{0:T(128)}, u32[]{:S(2)}) copy-start(f32[8]{0:T(128)} %param.21) | copy-start | bytes 100
  15.4 9.2 %collective-permute-start.1 = (f32[2,128,256]{2,1,0:T(8,128)S(1)}, f32[2,128,256]{2,1,0:T(8,128)S(1)}, u32[]{:S(2)}, u32[]{:S(2)}) collective-permute-start(f32[2,128,256]{2,1,0:T(8,128)S(1)} %maximum_select_fusion.1), channel_id=1, source_target_pairs={{0,4},{2,6},{4,0},{6,2},{8,12},{10,14},{12,8},{14,10},{16,20},{18,... | collective-permute-start | bytes 786440 | tf_op jit(solution)/shard_map/ppermute | solution.py:16
  20.9 1.4 copy-start.38
  21.2 0.8 copy-start.3
  24.7 0.8 copy-start.10
  28.4 0.8 copy-start
  28.4 2.4 %copy-start.20 = (f32[256,512]{1,0:T(8,128)S(1)}, f32[256,512]{1,0:T(8,128)}, u32[]{:S(2)}) copy-start(f32[256,512]{1,0:T(8,128)} %param.17) | copy-start | bytes 1572868
  29.2 119.2 %all-gather.7.cloned.1.call-start = ((), (), s32[]{:S(2)}) async-start(), calls=%async_computation.1 | async-start | bytes 1572864 | tf_op jit(solution)/shard_map/all_gather | solution.py:21
  70.2 1.2 copy-start.8
  70.3 0.9 copy-start.22
  71.3 1.7 copy-start.23
  73.0 1.0 copy-start.9
  88.4 1.2 copy-start.8
  88.5 0.9 copy-start.22
  89.4 1.7 copy-start.23
  91.1 1.0 copy-start.9
  94.8 10.5 %copy-start.21 = (f32[256,512]{1,0:T(8,128)S(1)}, f32[256,512]{1,0:T(8,128)}, u32[]{:S(2)}) copy-start(f32[256,512]{1,0:T(8,128)} %param.25) | copy-start | bytes 1572868
  97.2 4.3 %collective-permute-start.2 = (f32[256]{0:T(256)S(1)}, f32[256]{0:T(256)S(1)}, u32[]{:S(2)}, u32[]{:S(2)}) collective-permute-start(f32[256]{0:T(256)S(1)} %get-tuple-element.1425), channel_id=1, source_target_pairs={{0,2},{2,0},{4,6},{6,4},{8,10},{10,8},{12,14},{14,12},{16,18},{18,... | collective-permute-start | bytes 3080 | tf_op jit(solution)/shard_map/ppermute | solution.py:16
  101.5 4.8 %copy-start.31 = (f32[8,2,128]{2,0,1:T(8,128)S(1)}, f32[8,2,128]{2,0,1:T(8,128)}, u32[]{:S(2)}) copy-start(f32[8,2,128]{2,0,1:T(8,128)} %get-tuple-element.1459) | copy-start | bytes 24580
  101.5 5.9 %collective-permute-start.3 = (f32[256]{0:T(256)S(1)}, f32[256]{0:T(256)S(1)}, u32[]{:S(2)}, u32[]{:S(2)}) collective-permute-start(f32[256]{0:T(256)S(1)} %add.148), channel_id=1, source_target_pairs={{0,4},{2,6},{4,0},{6,2},{8,12},{10,14},{12,8},{14,10},{16,20},{18,... | collective-permute-start | bytes 3080 | tf_op jit(solution)/shard_map/ppermute | solution.py:16
  107.5 12.2 %copy-start.4 = (f32[256,512]{0,1:T(8,128)S(1)}, f32[256,512]{0,1:T(8,128)}, u32[]{:S(2)}) copy-start(f32[256,512]{0,1:T(8,128)} %copy-done.3) | copy-start | bytes 1572868
  109.6 4.3 %collective-permute-start.4 = (f32[256]{0:T(256)S(1)}, f32[256]{0:T(256)S(1)}, u32[]{:S(2)}, u32[]{:S(2)}) collective-permute-start(f32[256]{0:T(256)S(1)} %get-tuple-element.1298), channel_id=1, source_target_pairs={{0,2},{2,0},{4,6},{6,4},{8,10},{10,8},{12,14},{14,12},{16,18},{18,... | collective-permute-start | bytes 3080 | tf_op jit(solution)/shard_map/ppermute | solution.py:16
  113.9 5.8 %collective-permute-start.5 = (f32[256]{0:T(256)S(1)}, f32[256]{0:T(256)S(1)}, u32[]{:S(2)}, u32[]{:S(2)}) collective-permute-start(f32[256]{0:T(256)S(1)} %add.152), channel_id=1, source_target_pairs={{0,4},{2,6},{4,0},{6,2},{8,12},{10,14},{12,8},{14,10},{16,20},{18,... | collective-permute-start | bytes 3080 | tf_op jit(solution)/shard_map/ppermute | solution.py:16
  122.6 1.2 copy-start.11
  125.2 1.0 copy-start.6
  127.4 2.1 copy-start.13
  130.6 17.8 %copy-start.35 = (f32[8]{0:T(128)S(1)}, f32[8]{0:T(128)}, u32[]{:S(2)}) copy-start(f32[8]{0:T(128)} %get-tuple-element.1463) | copy-start | bytes 100
  152.7 4.7 %copy-start.1 = (f32[2,128,1,8,64]{1,4,3,2,0:T(8,128)}, f32[2,128,1,8,64]{1,4,3,2,0:T(8,128)S(1)}, u32[]{:S(2)}) copy-start(f32[2,128,1,8,64]{1,4,3,2,0:T(8,128)S(1)} %get-tuple-element.2071) | copy-start | bytes 1572868 | tf_op jit(solution)/shard_map/transpose(jvp())/while
  162.8 1.7 copy-start.26
  165.0 0.9 copy-start.16
  174.1 0.9 copy-start.14
  177.4 1.0 copy-start.2
  178.4 4.7 %copy-start.1 = (f32[2,128,1,8,64]{1,4,3,2,0:T(8,128)}, f32[2,128,1,8,64]{1,4,3,2,0:T(8,128)S(1)}, u32[]{:S(2)}) copy-start(f32[2,128,1,8,64]{1,4,3,2,0:T(8,128)S(1)} %get-tuple-element.2071) | copy-start | bytes 1572868 | tf_op jit(solution)/shard_map/transpose(jvp())/while
  188.5 1.7 copy-start.26
  190.8 0.9 copy-start.16
  199.9 0.9 copy-start.14
  203.1 1.0 copy-start.2
  204.2 1.1 copy-start.18
  205.3 5.5 %copy-start.12 = (f32[2,128,1,8,64]{1,0,4,3,2:T(2,128)S(1)}, f32[2,128,1,8,64]{1,0,4,3,2:T(2,128)}, u32[]{:S(2)}) copy-start(f32[2,128,1,8,64]{1,0,4,3,2:T(2,128)} %get-tuple-element.866) | copy-start | bytes 1572868
  205.4 3.9 %copy-start.28 = (f32[2,1,8,128]{3,2,1,0:T(8,128)S(1)}, f32[2,1,8,128]{3,2,1,0:T(8,128)}, u32[]{:S(2)}) copy-start(f32[2,1,8,128]{3,2,1,0:T(8,128)} %get-tuple-element.868) | copy-start | bytes 24580
  205.5 3.9 %copy-start.30 = (f32[8,256]{1,0:T(8,128)S(1)}, f32[8,256]{1,0:T(8,128)}, u32[]{:S(2)}) copy-start(f32[8,256]{1,0:T(8,128)} %param.18) | copy-start | bytes 24580
  205.5 5.3 %copy-start.7 = (f32[256,512]{0,1:T(8,128)S(1)}, f32[256,512]{0,1:T(8,128)}, u32[]{:S(2)}) copy-start(f32[256,512]{0,1:T(8,128)} %copy-done.5) | copy-start | bytes 1572868
  205.5 11.2 %collective-permute-start.6 = (f32[2,128,256]{2,1,0:T(8,128)S(1)}, f32[2,128,256]{2,1,0:T(8,128)S(1)}, u32[]{:S(2)}, u32[]{:S(2)}) collective-permute-start(f32[2,128,256]{2,1,0:T(8,128)S(1)} %broadcast_select_fusion), channel_id=1, source_target_pairs={{0,4},{2,6},{4,0},{6,2},{8,12},{10,14},{12,8},{14,10},{16,20},{18,... | collective-permute-start | bytes 786440 | tf_op jit(solution)/shard_map/ppermute | solution.py:16
  216.8 2.1 copy-start.42
  216.9 7.8 %collective-permute-start.7 = (f32[2,64,256]{2,1,0:T(8,128)S(1)}, f32[2,64,256]{2,1,0:T(8,128)S(1)}, u32[]{:S(2)}, u32[]{:S(2)}) collective-permute-start(f32[2,64,256]{2,1,0:T(8,128)S(1)} %slice_select_fusion), channel_id=1, source_target_pairs={{0,2},{2,0},{4,6},{6,4},{8,10},{10,8},{12,14},{14,12},{16,18},{18,... | collective-permute-start | bytes 393224 | tf_op jit(solution)/shard_map/ppermute | solution.py:16
  (28 other events, 18.7 us)
Sparse Core Ops, SparseCore 0:
  29.3 26.3 all-gather.4
  125.4 23.0 all-gather.6
where the time goes:
time: 235 us; the launch traced here: 232 us
  local copies, waits for them, and re-layouts  73.6 us (31%)
  waiting for transfers between devices  44.7 us (19%)
  matrix products  30.1 us (13%)
  starting transfers between devices  27 us (11%)
  other arithmetic  26.8 us (11%)
  between operations  15.4 us (7%)
  blocking collectives  14.1 us (6%)
    all_gather x2, waiting for transfers between devices, prefix(): pieces = jax.tree.map(lambda part: lax.all_gather(part, axis), value)  28.9 us
    dynamic_update_slice x12, local copies, waits for them, and re-layouts, stretch_scan(): lax.scan(stretch_advance, state_init, (x_blocks, to_blocks(step_size), to...  28.7 us
    ppermute x8, starting transfers between devices, from_partner(): lax.ppermute(shard, axis, [(i, i ^ 1 << apart) for i in range(lax.axis_si...  27 us
    unnamed x71, local copies, waits for them, and re-layouts  15.7 us
    ppermute x8, waiting for transfers between devices, from_partner(): lax.ppermute(shard, axis, [(i, i ^ 1 << apart) for i in range(lax.axis_si...  15.7 us
    while x72, local copies, waits for them, and re-layouts  12.6 us
    dot_general x6, matrix products, stretch_advance(): inner = jnp.einsum('ghij,jghp->ighp', mixing, scaled_x, precision=HIGH)  10.4 us
    unnamed x1, blocking collectives  10.1 us
  transfers between devices with their start and end apart: 10, of which 9 were waited for; matrix products, arithmetic and copies ran while one was open for 6% of the time, Pallas kernels for 0%

commit v1 on v0

v1 whole, which is shorter than its diff:
```python
import jax
import jax.numpy as jnp
from jax import lax
from jax.experimental import pallas as pl
from jax.experimental.pallas import tpu as pltpu
from jax.sharding import PartitionSpec as P

MESH = pl.DeviceIdType.MESH
F32 = jnp.float32
BF = jnp.bfloat16
T = 256
Q = 128
N = 256
D = 512
H = 8
W = 64
ROWS = 16
TILES = T // ROWS
GROUP_WIDTH = 2048
EPSILON = 1e-05

NN = (((1,), (0,)), ((), ()))
NT = (((1,), (1,)), ((), ()))


def halves(v):
    hi = v.astype(BF)
    return hi, (v - hi.astype(F32)).astype(BF)


def dot(a, b, dims=NN):
    return lax.dot_general(a, b, dims, preferred_element_type=F32)


def dot3(a, b, dims=NN):
    return dot(a[0], b[0], dims) + (dot(a[0], b[1], dims) + dot(a[1], b[0], dims))


def thirds(v):
    hi = v.astype(BF).astype(F32)
    mid = (v - hi).astype(BF).astype(F32)
    return jnp.concatenate([hi, mid, v - hi - mid, jnp.zeros_like(v)], axis=0)


def sum_thirds(v):
    return v[0:8] + (v[8:16] + v[16:24])


def lanes(v):
    return (v[:, 0:128] + v[:, 128:256]) + (v[:, 256:384] + v[:, 384:512])


def fold(v):
    return v[0:8] + v[8:16]


def tiles(step, count=TILES, init=None):
    def run(i, carry):
        return step(pl.ds(pl.multiple_of(i * ROWS, ROWS), ROWS), carry)

    return lax.fori_loop(0, count, run, 0 if init is None else init)


def iota(shape, dim):
    return lax.broadcasted_iota(jnp.int32, shape, dim)


def body(
    x_in, z_in, raw_in, b_in, c_in, decay_s, bias_s, skip_s, gain_in, og_in,
    out_o, hg_o, zg_o, sg_o, bg_o, cg_o, decay_o, bias_o, skip_o, gain_o,
    xv, zv, ogv, rawv, gainv, bv, cv,
    a1, a2, a5, gate, dgate, ogg, vh, vl, kh, kl, ph, pld,
    bh, bl, ch, cl, cth, ctl, bth, btl, gh, gl, gth, gtl,
    state, other, yi, yv, gated, qh, ql, norm, cols, dy, uh, ul, sh, sl, rh, rl,
    dv, dx, first, second, recv_a, recv_b, small, outv, hgv, zgv, sgv,
    local_sem, send_sem, recv_sem,
):
    dp = lax.axis_index("dp")
    ctx = lax.axis_index("ctx")
    place = lax.rem(dp, 4)
    base = dp - place
    right = base + lax.rem(place + 1, 4)
    left = base + lax.rem(place + 3, 4)
    across = base + lax.rem(place + 2, 4)
    early = ctx == 0
    late = ctx == 1

    used = []

    def local(src, dst):
        copy = pltpu.make_async_copy(src, dst, local_sem.at[len(used)])
        used.append(copy)
        return copy

    sent = []

    def remote(src, dst, device):
        k = len(sent)
        sent.append(k)
        return pltpu.make_async_remote_copy(
            src_ref=src, dst_ref=dst, send_sem=send_sem.at[k], recv_sem=recv_sem.at[k],
            device_id=device, device_id_type=MESH,
        )

    to_right, to_left, to_across, to_core = (right, ctx), (left, ctx), (across, ctx), (dp, 1 - ctx)

    barrier = pltpu.get_barrier_semaphore()
    for device in (to_right, to_left, to_across, to_core):
        pl.semaphore_signal(barrier, inc=1, device_id=device, device_id_type=MESH)

    get_raw = local(raw_in, rawv)
    get_gain = local(gain_in, gainv.at[0])
    get_x = local(x_in, xv)
    get_z = local(z_in, zv)
    get_og = local(og_in, ogv)
    get_b = local(b_in, bv.at[pl.ds(0, W)])
    get_c = local(c_in, cv.at[pl.ds(0, W)])
    for copy in used:
        copy.start()
    pl.semaphore_wait(barrier, 4)

    b_right = remote(b_in, bv.at[pl.ds(W, W)], to_right)
    b_left = remote(b_in, bv.at[pl.ds(2 * W, W)], to_left)
    c_right = remote(c_in, cv.at[pl.ds(W, W)], to_right)
    c_left = remote(c_in, cv.at[pl.ds(2 * W, W)], to_left)
    half = W // 2
    b_on_right = remote(bv.at[pl.ds(W, half)], bv.at[pl.ds(3 * W, half)], to_right)
    b_on_left = remote(bv.at[pl.ds(2 * W + half, half)], bv.at[pl.ds(3 * W + half, half)], to_left)
    c_on_right = remote(cv.at[pl.ds(W, half)], cv.at[pl.ds(3 * W, half)], to_right)
    c_on_left = remote(cv.at[pl.ds(2 * W + half, half)], cv.at[pl.ds(3 * W + half, half)], to_left)
    for copy in (b_right, b_left, c_right, c_left):
        copy.start()

    def per_head(ref, width):
        row = iota((H, width), 0)
        value = jnp.full((H, width), ref[0], F32)
        for h in range(1, H):
            value = jnp.where(row == h, ref[h], value)
        return value

    get_raw.wait()
    speed = jnp.exp(per_head(decay_s, T))
    pre = rawv[...] + per_head(bias_s, T)
    step = jnp.maximum(pre, 0.0) + jnp.log1p(jnp.exp(-jnp.abs(pre)))
    rate = -speed * step
    src, dst = iota((T, T), 0), iota((T, T), 1)
    upto = jnp.where((src <= dst) & (src // Q == dst // Q), 1.0, 0.0).astype(BF)
    run = sum_thirds(dot(thirds(rate).astype(BF), upto))
    total0 = run[:, Q - 1:Q]
    total1 = run[:, T - 1:T]
    position = iota((H, T), 1)
    block1 = position >= Q
    centre = 0.5 * jnp.where(block1, total1, total0)
    scale1 = jnp.exp(run - centre)
    scale2 = step * jnp.exp(centre - run)
    since_start = jnp.where(block1, run + total0, run)
    to_end = jnp.where(block1, total1 - run, total0 - run + total1)
    scale5 = jnp.where(early, step, 1.0) * jnp.exp(jnp.where(early, to_end, since_start))
    stacked = jnp.concatenate(
        [thirds(scale1), thirds(scale2), thirds(scale5), jnp.zeros((32, T), F32)], axis=0
    ).T.astype(BF)
    row, col = iota((128, D), 0), iota((128, D), 1)
    same = (row % 8 == col // W) & (row % 32 < 24)
    for k, ref in enumerate((a1, a2, a5)):
        spread = jnp.where(same & (row // 32 == k), 1.0, 0.0).astype(BF)
        ref[...] = dot(stacked, spread)
    own = iota((H, D), 0) == iota((H, D), 1) // W
    kappa = jnp.sum(
        jnp.where(own, jnp.exp(0.5 * (total0 + total1)), 0.0), axis=0, keepdims=True
    )
    skip_row = jnp.sum(jnp.where(own, per_head(skip_s, D), 0.0), axis=0, keepdims=True)

    get_gain.wait()
    get_x.wait()
    get_z.wait()
    get_og.wait()

    def prepare(r, carry):
        z = zv[r]
        sig = 1.0 / (1.0 + jnp.exp(-z))
        gate[r] = z * sig
        dgate[r] = sig * (1.0 + z * (1.0 - sig))
        ogg[r] = ogv[r] * gainv[...]
        x = xv[r]
        vh[r], vl[r] = halves(a2[r] * x)
        ph[r], pld[r] = halves(a5[r] * x)
        return carry

    tiles(prepare)

    def prepare0(r, carry):
        kh[r], kl[r] = halves((a2[r] * xv[r]) * kappa)
        return carry

    tiles(prepare0, TILES // 2)

    b_right.wait_recv()
    b_on_right.start()
    b_left.wait_recv()
    b_on_left.start()
    c_right.wait_recv()
    c_on_right.start()
    c_left.wait_recv()
    c_on_left.start()
    get_b.wait()
    get_c.wait()
    b_on_right.wait_recv()
    b_on_left.wait_recv()
    bh[...], bl[...] = halves(bv[...])

    state_out = [remote(state.at[k], other.at[k], to_core) for k in range(2)]

    @pl.when(early)
    def _():
        for k in range(2):
            part = pl.ds(k * 256, 256)
            state[k] = dot3((bh[...], bl[...]), (ph[:, part], pld[:, part]))
            state_out[k].start()

    c_on_right.wait_recv()
    c_on_left.wait_recv()
    cth[...], ctl[...] = halves(cv[...].T)
    ch[...], cl[...] = halves(cv[...])

    low = src >= dst
    g0 = dot3((cth[0:Q], ctl[0:Q]), (bh[:, 0:Q], bl[:, 0:Q]))
    g1 = dot3((cth[Q:T], ctl[Q:T]), (bh[...], bl[...]))
    g0 = jnp.where(low[0:Q, 0:Q], g0, 0.0)
    g1 = jnp.where(low[Q:T], g1, 0.0)
    gh[0:Q, 0:Q], gl[0:Q, 0:Q] = halves(g0)
    gh[Q:T], gl[Q:T] = halves(g1)
    gth[0:Q, 0:Q], gtl[0:Q, 0:Q] = halves(g0.T)
    gth[:, Q:T], gtl[:, Q:T] = halves(g1.T)
    for k in range(2):
        part = pl.ds(k * 256, 256)
        yi[0:Q, part] = dot3((gh[0:Q, 0:Q], gl[0:Q, 0:Q]), (vh[0:Q, part], vl[0:Q, part]))
        yi[Q:T, part] = dot3(
            (gh[Q:T], gl[Q:T]),
            (
                jnp.concatenate([kh[:, part], vh[Q:T, part]], axis=0),
                jnp.concatenate([kl[:, part], vl[Q:T, part]], axis=0),
            ),
        )

    def mix(r, y):
        yv[r] = y
        mixed = y + skip_row * xv[r]
        g = mixed * gate[r]
        gated[r] = g
        qh[r, 0:128], ql[r, 0:128] = halves(lanes(g * g))
        qh[r, 128:256], ql[r, 128:256] = halves(lanes(g * ogg[r]))

    @pl.when(early)
    def _():
        def go(r, carry):
            mix(r, a1[r] * yi[r])
            return carry

        tiles(go)
        bth[...], btl[...] = halves(bv[...].T)

    @pl.when(late)
    def _():
        for k in range(2):
            state_out[k].wait_recv()
            sh[k], sl[k] = halves(other[k])
            dx[:, pl.ds(k * 256, 256)] = dot3((cth[...], ctl[...]), (sh[k], sl[k]))

        def go(r, carry):
            mix(r, a1[r] * yi[r] + a5[r] * dx[r])
            return carry

        tiles(go)

    pick = jnp.where(iota((H, 256), 0) == iota((H, 256), 1) // 128, 1.0, 0.0).astype(BF)
    norm[0] = dot(pick, qh[:, 0:256], NT) + dot(pick, ql[:, 0:256], NT)
    norm_out = [
        remote(norm.at[0], norm.at[1 + k], device)
        for k, device in enumerate((to_right, to_left, to_across))
    ]
    for copy in norm_out:
        copy.start()
    for copy in norm_out:
        copy.wait_recv()
    sums = (norm[0] + norm[1]) + (norm[2] + norm[3])
    inverse = lax.rsqrt(sums[0:1] * (1.0 / GROUP_WIDTH) + EPSILON)
    slope = inverse * inverse * inverse * sums[1:2] * (1.0 / GROUP_WIDTH)
    lead = iota((128, T), 0)
    cols[...] = jnp.where(lead == 0, inverse, jnp.where(lead == 1, slope, 0.0)).T

    def finish(r, carry):
        gain_sum, skip_sum = carry
        inv = cols[r, 0:1]
        k = cols[r, 1:2]
        g = gated[r]
        x = xv[r]
        y = yv[r]
        normed = g * inv
        outv[r] = normed * gainv[...]
        grad = ogg[r] * inv - g * k
        zgv[r] = grad * (y + skip_row * x) * dgate[r]
        d = grad * gate[r]
        dy[r] = d
        uh[r], ul[r] = halves(a1[r] * d)
        qh[r], ql[r] = halves(d * y)
        return gain_sum + fold(ogv[r] * normed), skip_sum + fold(d * x)

    zero = jnp.zeros((8, D), F32)
    gain_sum, skip_sum = tiles(finish, init=(zero, zero))
    put_out = local(outv, out_o)
    put_zg = local(zgv, zg_o)
    put_out.start()
    put_zg.start()

    start_out = [remote(state.at[k], other.at[k], to_core) for k in range(2)]

    @pl.when(late)
    def _():
        def go(r, carry):
            ph[r], pld[r] = halves(a5[r] * dy[r])
            return carry

        tiles(go)
        for k in range(2):
            part = pl.ds(k * 256, 256)
            state[k] = dot3((ch[...], cl[...]), (ph[:, part], pld[:, part]))
            start_out[k].start()

    d0 = dot3((uh[0:Q], ul[0:Q]), (vh[0:Q], vl[0:Q]), NT)
    d10 = dot3((uh[Q:T], ul[Q:T]), (kh[...], kl[...]), NT)
    d11 = dot3((uh[Q:T], ul[Q:T]), (vh[Q:T], vl[Q:T]), NT)
    diagonal = low[0:Q, 0:Q]
    gh[0:Q, 0:Q], gl[0:Q, 0:Q] = halves(jnp.where(diagonal, d0, 0.0))
    gh[0:Q, Q:T] = jnp.zeros((Q, Q), BF)
    gl[0:Q, Q:T] = jnp.zeros((Q, Q), BF)
    gh[Q:T, 0:Q], gl[Q:T, 0:Q] = halves(d10)
    gh[Q:T, Q:T], gl[Q:T, Q:T] = halves(jnp.where(diagonal, d11, 0.0))

    def c_part():
        return dot3((bh[...], bl[...]), (gh[...], gl[...]), NT)

    def b_part():
        return dot3((ch[...], cl[...]), (gh[...], gl[...]))

    def scatter(full, landing):
        far_right = remote(full.at[pl.ds(3 * W, half)], landing.at[pl.ds(0, half)], to_right)
        far_left = remote(full.at[pl.ds(3 * W + half, half)], landing.at[pl.ds(half, half)], to_left)
        near_right = remote(full.at[pl.ds(2 * W + half, half)], landing.at[pl.ds(W + half, half)], to_right)
        near_left = remote(full.at[pl.ds(W, half)], landing.at[pl.ds(2 * W, half)], to_left)
        sum_right = remote(full.at[pl.ds(2 * W, half)], landing.at[pl.ds(W, half)], to_right)
        sum_left = remote(full.at[pl.ds(W + half, half)], landing.at[pl.ds(2 * W + half, half)], to_left)

        def start():
            for copy in (far_right, far_left, near_right, near_left):
                copy.start()

        def relay():
            far_right.wait_recv()
            full[pl.ds(2 * W, half)] += landing[pl.ds(0, half)]
            sum_right.start()
            far_left.wait_recv()
            full[pl.ds(W + half, half)] += landing[pl.ds(half, half)]
            sum_left.start()

        def end():
            for copy in (near_right, near_left, sum_right, sum_left):
                copy.wait_recv()
            full[0:W] += landing[W:2 * W] + landing[2 * W:3 * W]
            for copy in (far_right, far_left, near_right, near_left, sum_right, sum_left):
                copy.wait_send()

        return start, relay, end

    first_start, first_relay, first_end = scatter(first, recv_a)
    second_start, second_relay, second_end = scatter(second, recv_b)

    @pl.when(early)
    def _():
        first[...] = c_part()
        first_start()
        second[...] = b_part()

    @pl.when(late)
    def _():
        first[...] = b_part()
        first_start()
        second[...] = c_part() + (
            dot3((sh[0], sl[0]), (ph[:, 0:256], pld[:, 0:256]), NT)
            + dot3((sh[1], sl[1]), (ph[:, 256:512], pld[:, 256:512]), NT)
        )
        second_start()

    for k in range(2):
        part = pl.ds(k * 256, 256)
        dv[0:Q, part] = dot3((gth[0:Q, 0:Q], gtl[0:Q, 0:Q]), (uh[0:Q, part], ul[0:Q, part])) + kappa[
            :, k * 256:(k + 1) * 256
        ] * dot3((gth[0:Q, Q:T], gtl[0:Q, Q:T]), (uh[Q:T, part], ul[Q:T, part]))
        dv[Q:T, part] = dot3((gth[Q:T, Q:T], gtl[Q:T, Q:T]), (uh[Q:T, part], ul[Q:T, part]))

    first_relay()

    @pl.when(early)
    def _():
        for k in range(2):
            start_out[k].wait_recv()
            rh[k], rl[k] = halves(other[k])
        second[...] += dot3((rh[0], rl[0]), (ph[:, 0:256], pld[:, 0:256]), NT) + dot3(
            (rh[1], rl[1]), (ph[:, 256:512], pld[:, 256:512]), NT
        )
        second_start()
        for k in range(2):
            dx[:, pl.ds(k * 256, 256)] = dot3((bth[...], btl[...]), (rh[k], rl[k]))

    def gather_x(r, f):
        hgv[r] = f + skip_row * dy[r]
        sxh, sxl = halves(f * xv[r])
        uh[r] = sxh
        ul[r] = sxl

    small[0:16] = jnp.zeros((16, D), F32)

    @pl.when(early)
    def _():
        def go(r, carry):
            gather_x(r, a2[r] * dv[r] + a5[r] * dx[r])
            return carry

        tiles(go)
        sums = []
        for k in range(2):
            sums.append(tiles(
                lambda r, acc, k=k: acc + fold(state[k, r] * other[k, r]),
                init=jnp.zeros((8, 256), F32),
            ))
        small[8:16] = jnp.concatenate(sums, axis=1)

    @pl.when(late)
    def _():
        def go(r, carry):
            gather_x(r, a2[r] * dv[r])
            return carry

        tiles(go)

    put_hg = local(hgv, hg_o)
    put_hg.start()
    second_relay()

    heads = jnp.where(own, 1.0, 0.0).astype(BF)
    y_sum = dot(heads, qh[...], NT) + dot(heads, ql[...], NT)
    x_sum = dot(heads, uh[...], NT) + dot(heads, ul[...], NT)
    from_end = jnp.sum(
        jnp.where(own, jnp.sum(small[8:16], axis=0, keepdims=True), 0.0), axis=1, keepdims=True
    )
    onward = jnp.where(low, 1.0, 0.0).astype(BF)
    rate_grad = sum_thirds(dot(thirds(y_sum - x_sum).astype(BF), onward)) + from_end
    step_grad = (x_sum / step - speed * rate_grad) * (1.0 / (1.0 + jnp.exp(-pre)))
    sgv[...] = step_grad
    put_sg = local(sgv, sg_o)
    put_sg.start()

    def as_row(column):
        hit = iota((H, D), 0) == iota((H, D), 1)
        return jnp.sum(jnp.where(hit, column, 0.0), axis=0, keepdims=True)

    skip_column = jnp.sum(
        jnp.where(own, jnp.sum(skip_sum, axis=0, keepdims=True), 0.0), axis=1, keepdims=True
    )
    small[0:1] = jnp.sum(gain_sum, axis=0, keepdims=True)
    small[1:2] = as_row(jnp.sum(rate_grad * rate, axis=1, keepdims=True))
    small[2:3] = as_row(jnp.sum(step_grad, axis=1, keepdims=True))
    small[3:4] = as_row(skip_column)
    small_out = remote(small.at[pl.ds(0, 8)], small.at[pl.ds(16, 8)], to_core)
    small_out.start()
    first_end()

    put_first = [local(first.at[pl.ds(0, W)], o) for o in (cg_o, bg_o)]
    put_second = [local(second.at[pl.ds(0, W)], o) for o in (bg_o, cg_o)]

    @pl.when(early)
    def _():
        put_first[0].start()

    @pl.when(late)
    def _():
        put_first[1].start()

    small_out.wait()
    small[24:32] = small[0:8] + small[16:24]
    put_small = [local(small.at[24, pl.ds(0, D)], gain_o)]
    for k, ref in enumerate((decay_o, bias_o, skip_o)):
        ref[...] = small[25 + k, 0:H]
    for copy in put_small:
        copy.start()
    second_end()

    @pl.when(early)
    def _():
        put_second[0].start()
        put_first[0].wait()
        put_second[0].wait()
        for k in range(2):
            state_out[k].wait_send()

    @pl.when(late)
    def _():
        put_second[1].start()
        put_first[1].wait()
        put_second[1].wait()
        for k in range(2):
            start_out[k].wait_send()

    for copy in [put_out, put_zg, put_hg, put_sg] + put_small:
        copy.wait()
    for copy in [b_right, b_left, c_right, c_left, b_on_right, b_on_left, c_on_right, c_on_left] + norm_out:
        copy.wait_send()


def shards(*args):
    def f32(*shape):
        return jax.ShapeDtypeStruct(shape, F32)

    def vm(*shape):
        return pltpu.VMEM(shape, F32)

    def vb(*shape):
        return pltpu.VMEM(shape, BF)

    anywhere = pl.BlockSpec(memory_space=pl.ANY)
    scalars = pl.BlockSpec(memory_space=pltpu.SMEM)
    scratch = [
        vm(T, D), vm(T, D), vm(T, D), vm(H, T), vm(1, D), vm(N, T), vm(N, T),
        vm(T, D), vm(T, D), vm(T, D), vm(T, D), vm(T, D), vm(T, D),
        vb(T, D), vb(T, D), vb(Q, D), vb(Q, D), vb(T, D), vb(T, D),
        vb(N, T), vb(N, T), vb(N, T), vb(N, T), vb(T, N), vb(T, N), vb(T, N), vb(T, N),
        vb(T, T), vb(T, T), vb(T, T), vb(T, T),
        vm(2, N, 256), vm(2, N, 256), vm(T, D), vm(T, D), vm(T, D), vb(T, D), vb(T, D),
        vm(4, 8, T), vm(T, 128), vm(T, D), vb(T, D), vb(T, D),
        vb(2, N, 256), vb(2, N, 256), vb(2, N, 256), vb(2, N, 256),
        vm(T, D), vm(T, D), vm(N, T), vm(N, T), vm(3 * W, T), vm(3 * W, T), vm(32, D),
        vm(T, D), vm(T, D), vm(T, D), vm(H, T),
        pltpu.SemaphoreType.DMA((24,)),
        pltpu.SemaphoreType.DMA((28,)),
        pltpu.SemaphoreType.DMA((28,)),
    ]
    return pl.pallas_call(
        body,
        out_shape=[
            f32(T, D), f32(T, D), f32(T, D), f32(H, T), f32(W, T), f32(W, T),
            f32(H), f32(H), f32(H), f32(D),
        ],
        in_specs=[anywhere] * 5 + [scalars] * 3 + [anywhere] * 2,
        out_specs=[anywhere] * 6 + [pl.BlockSpec(memory_space=pltpu.VMEM)] * 3 + [anywhere],
        scratch_shapes=scratch,
        compiler_params=pltpu.CompilerParams(
            collective_id=0, has_side_effects=True, vmem_limit_bytes=48 * 1024 * 1024
        ),
        name="layer",
    )(*args)


def solution(mesh):
    rows, cols = P("ctx", "dp"), P("dp", "ctx")
    heads = P("dp")
    return jax.shard_map(
        shards,
        mesh=mesh,
        in_specs=(rows, rows, cols, cols, cols, heads, heads, heads, heads, rows),
        out_specs=(rows, rows, rows, cols, cols, cols, heads, heads, heads, heads),
        check_vma=False,
    )
```

time: 235 us -> 50.7 us (0.22); the launches traced: 232 us -> 50.2 us
  local copies, waits for them, and re-layouts: 73.6 us -> 14.5 us
  waiting for transfers between devices: 44.7 us -> 0 us
  Pallas kernels: 0 us -> 35.1 us
  matrix products: 30.1 us -> 0 us
  starting transfers between devices: 27 us -> 0 us
  other arithmetic: 26.8 us -> 0 us
  between operations: 15.4 us -> 0.68 us
  blocking collectives: 14.1 us -> 0 us
    pallas_call x0 -> x1, Pallas kernels: none -> 35.1 us  [shards(): pl.pallas_call(body, out_shape=[f32(T, D), f32(T, D), f32(T, D), f32(H, T...]
    dot_general x27 -> x0, matrix products: 30.1 us -> none  [the longest x6 10.4 us: stretch_advance(): inner = jnp.einsum('ghij,jghp->ighp', mixing, scaled_x, precision=HIGH)]
    all_gather x2 -> x0, waiting for transfers between devices: 28.9 us -> none  [prefix(): pieces = jax.tree.map(lambda part: lax.all_gather(part, axis), value)]
    dynamic_update_slice x12 -> x0, local copies, waits for them, and re-layouts: 28.7 us -> none  [stretch_scan(): lax.scan(stretch_advance, state_init, (x_blocks, to_blocks(step_size), to...]
    ppermute x8 -> x0, starting transfers between devices: 27 us -> none  [from_partner(): lax.ppermute(shard, axis, [(i, i ^ 1 << apart) for i in range(lax.axis_si...]
    ppermute x8 -> x0, waiting for transfers between devices: 15.7 us -> none  [from_partner(): lax.ppermute(shard, axis, [(i, i ^ 1 << apart) for i in range(lax.axis_si...]
    while x72 -> x0, local copies, waits for them, and re-layouts: 12.6 us -> none
    reduce_sum x13 -> x0, other arithmetic: 11.3 us -> none  [the longest x2 2.99 us: shards(): jnp.sum((mixed_grad * head_inputs).reshape(length, local_heads, P_SIZE),...]
  transfers between devices with their start and end apart: 10 -> 0, of which waited for: 9 -> 0; matrix products, arithmetic and copies ran while one was open for 6% -> 0% of each run, Pallas kernels for 0% -> 0%
where the time goes in v1:
time: 50.7 us; the launch traced here: 50.2 us
  Pallas kernels  35.1 us (69%)
  local copies, waits for them, and re-layouts  14.5 us (29%)
  between operations  0.68 us (1%)
    pallas_call x1, Pallas kernels, shards(): pl.pallas_call(body, out_shape=[f32(T, D), f32(T, D), f32(T, D), f32(H, T...  35.1 us
    unnamed x30, local copies, waits for them, and re-layouts  14.5 us

profile of v1, /device:TPU:1, one launch (start us, length us, event | category | flops | bytes accessed | tf_op | source)
XLA Modules:
  0.0 50.2 jit_solution(6566693474077813257)
XLA Ops:
  0.6 0.0 copy-start
  0.7 1.0 %copy-done = f32[256,512]{1,0:T(8,128)S(1)} copy-done((f32[256,512]{1,0:T(8,128)S(1)}, f32[256,512]{1,0:T(8,128)}, u32[]{:S(2)}) %copy-start) | copy-done | bytes 524312
  1.7 0.0 copy-start.1
  1.7 1.0 %copy-done.1 = f32[256,512]{1,0:T(8,128)S(1)} copy-done((f32[256,512]{1,0:T(8,128)S(1)}, f32[256,512]{1,0:T(8,128)}, u32[]{:S(2)}) %copy-start.1) | copy-done | bytes 524312
  2.7 0.0 copy-start.2
  2.7 1.0 %copy-done.2 = f32[256,512]{1,0:T(8,128)S(1)} copy-done((f32[256,512]{1,0:T(8,128)S(1)}, f32[256,512]{1,0:T(8,128)}, u32[]{:S(2)}) %copy-start.2) | copy-done | bytes 524312
  3.8 0.0 copy-start.3
  3.8 0.8 %copy-done.3 = f32[64,256]{1,0:T(8,128)S(1)} copy-done((f32[64,256]{1,0:T(8,128)S(1)}, f32[64,256]{1,0:T(8,128)}, u32[]{:S(2)}) %copy-start.3) | copy-done | bytes 65560
  4.6 0.0 copy-start.4
  4.6 0.8 %copy-done.4 = f32[64,256]{1,0:T(8,128)S(1)} copy-done((f32[64,256]{1,0:T(8,128)S(1)}, f32[64,256]{1,0:T(8,128)}, u32[]{:S(2)}) %copy-start.4) | copy-done | bytes 65560
  5.5 0.0 copy-start.5
  5.5 0.7 %copy-done.5 = f32[8,256]{1,0:T(8,128)S(1)} copy-done((f32[8,256]{1,0:T(8,128)S(1)}, f32[8,256]{1,0:T(8,128)}, u32[]{:S(2)}) %copy-start.5) | copy-done | bytes 8216
  6.2 0.0 copy-start.6
  6.2 0.7 %copy-done.6 = f32[512]{0:T(512)S(1)} copy-done((f32[512]{0:T(512)S(1)}, f32[512]{0:T(512)}, u32[]{:S(2)}) %copy-start.6) | copy-done | bytes 2072
  6.8 0.0 copy-start.7
  6.8 0.7 %copy-done.7 = f32[8]{0:T(128)S(1)} copy-done((f32[8]{0:T(128)S(1)}, f32[8]{0:T(128)}, u32[]{:S(2)}) %copy-start.7) | copy-done | bytes 56
  7.5 0.0 copy-start.8
  7.5 0.7 %copy-done.8 = f32[8]{0:T(128)S(1)} copy-done((f32[8]{0:T(128)S(1)}, f32[8]{0:T(128)}, u32[]{:S(2)}) %copy-start.8) | copy-done | bytes 56
  8.1 0.0 copy-start.9
  8.1 0.7 %copy-done.9 = f32[8]{0:T(128)S(1)} copy-done((f32[8]{0:T(128)S(1)}, f32[8]{0:T(128)}, u32[]{:S(2)}) %copy-start.9) | copy-done | bytes 56
  8.8 35.1 %layer.1 = (f32[256,512]{1,0:T(8,128)S(1)}, f32[256,512]{1,0:T(8,128)S(1)}, f32[256,512]{1,0:T(8,128)S(1)}, f32[8,256]{1,0:T(8,128)S(1)}, f32[64,256]{1,0:T(8,12...) custom-call(f32[256,512]{1,0:T(8,128)S(1)} %copy-done, ...), custom_call_target="tpu_custom_call" | custom-call | tf_op jit(solution)/shard_map/layer/pallas_call | solution.py:546
  43.9 0.8 %copy.30 = f32[256,512]{1,0:T(8,128)} copy(f32[256,512]{1,0:T(8,128)S(1)} %get-tuple-element.20) | data formatting | bytes 1048576
  44.7 0.8 %copy.31 = f32[256,512]{1,0:T(8,128)} copy(f32[256,512]{1,0:T(8,128)S(1)} %get-tuple-element.21) | data formatting | bytes 1048576
  45.5 0.8 %copy.32 = f32[256,512]{1,0:T(8,128)} copy(f32[256,512]{1,0:T(8,128)S(1)} %get-tuple-element.22) | data formatting | bytes 1048576
  46.3 0.6 %copy.33 = f32[8,256]{1,0:T(8,128)} copy(f32[8,256]{1,0:T(8,128)S(1)} %get-tuple-element.23) | data formatting | bytes 16384
  46.9 0.6 %copy.34 = f32[64,256]{1,0:T(8,128)} copy(f32[64,256]{1,0:T(8,128)S(1)} %get-tuple-element.24) | data formatting | bytes 131072
  47.5 0.6 %copy.35 = f32[64,256]{1,0:T(8,128)} copy(f32[64,256]{1,0:T(8,128)S(1)} %get-tuple-element.25) | data formatting | bytes 131072
  48.1 0.5 %copy.36 = f32[8]{0:T(128)} copy(f32[8]{0:T(128)S(1)} %get-tuple-element.26) | data formatting | bytes 64
  48.6 0.5 %copy.37 = f32[8]{0:T(128)} copy(f32[8]{0:T(128)S(1)} %get-tuple-element.27) | data formatting | bytes 64
  49.1 0.5 %copy.38 = f32[8]{0:T(128)} copy(f32[8]{0:T(128)S(1)} %get-tuple-element.28) | data formatting | bytes 64
  49.7 0.6 %copy.39 = f32[512]{0:T(512)} copy(f32[512]{0:T(512)S(1)} %get-tuple-element.29) | data formatting | bytes 4096
Async XLA Ops:
  0.6 1.0 %copy-start = (f32[256,512]{1,0:T(8,128)S(1)}, f32[256,512]{1,0:T(8,128)}, u32[]{:S(2)}) copy-start(f32[256,512]{1,0:T(8,128)} %x_in.1) | copy-start | bytes 1572868
  1.7 1.0 %copy-start.1 = (f32[256,512]{1,0:T(8,128)S(1)}, f32[256,512]{1,0:T(8,128)}, u32[]{:S(2)}) copy-start(f32[256,512]{1,0:T(8,128)} %z_in.1) | copy-start | bytes 1572868
  2.7 1.0 %copy-start.2 = (f32[256,512]{1,0:T(8,128)S(1)}, f32[256,512]{1,0:T(8,128)}, u32[]{:S(2)}) copy-start(f32[256,512]{1,0:T(8,128)} %og_in.1) | copy-start | bytes 1572868
  3.8 0.8 %copy-start.3 = (f32[64,256]{1,0:T(8,128)S(1)}, f32[64,256]{1,0:T(8,128)}, u32[]{:S(2)}) copy-start(f32[64,256]{1,0:T(8,128)} %b_in.1) | copy-start | bytes 196612
  4.6 0.8 %copy-start.4 = (f32[64,256]{1,0:T(8,128)S(1)}, f32[64,256]{1,0:T(8,128)}, u32[]{:S(2)}) copy-start(f32[64,256]{1,0:T(8,128)} %c_in.1) | copy-start | bytes 196612
  5.5 0.7 %copy-start.5 = (f32[8,256]{1,0:T(8,128)S(1)}, f32[8,256]{1,0:T(8,128)}, u32[]{:S(2)}) copy-start(f32[8,256]{1,0:T(8,128)} %raw_in.1) | copy-start | bytes 24580
  6.2 0.7 %copy-start.6 = (f32[512]{0:T(512)S(1)}, f32[512]{0:T(512)}, u32[]{:S(2)}) copy-start(f32[512]{0:T(512)} %gain_in.1) | copy-start | bytes 6148
  6.8 0.7 %copy-start.7 = (f32[8]{0:T(128)S(1)}, f32[8]{0:T(128)}, u32[]{:S(2)}) copy-start(f32[8]{0:T(128)} %decay_s.1) | copy-start | bytes 100
  7.5 0.7 %copy-start.8 = (f32[8]{0:T(128)S(1)}, f32[8]{0:T(128)}, u32[]{:S(2)}) copy-start(f32[8]{0:T(128)} %bias_s.1) | copy-start | bytes 100
  8.1 0.7 %copy-start.9 = (f32[8]{0:T(128)S(1)}, f32[8]{0:T(128)}, u32[]{:S(2)}) copy-start(f32[8]{0:T(128)} %skip_s.1) | copy-start | bytes 100

commit v2 on v1

--- a/solution.py
+++ b/solution.py
@@ -66,9 +66,9 @@
 
 
 def body(
-    x_in, z_in, raw_in, b_in, c_in, decay_s, bias_s, skip_s, gain_in, og_in,
-    out_o, hg_o, zg_o, sg_o, bg_o, cg_o, decay_o, bias_o, skip_o, gain_o,
-    xv, zv, ogv, rawv, gainv, bv, cv,
+    x_in, z_in, raw_in, b_in, c_in, decay_in, bias_in, skip_in, gain_in, og_in,
+    out_o, hg_o, zg_o, sg_o, bg_o, cg_o, params_o,
+    xv, zv, ogv, rawv, gainv, decay_s, bias_s, skip_s, bv, cv,
     a1, a2, a5, gate, dgate, ogg, vh, vl, kh, kl, ph, pld,
     bh, bl, ch, cl, cth, ctl, bth, btl, gh, gl, gth, gtl,
     state, other, yi, yv, gated, qh, ql, norm, cols, dy, uh, ul, sh, sl, rh, rl,
@@ -108,6 +108,10 @@
     for device in (to_right, to_left, to_across, to_core):
         pl.semaphore_signal(barrier, inc=1, device_id=device, device_id_type=MESH)
 
+    get_heads = [
+        local(ref, row)
+        for ref, row in ((decay_in, decay_s), (bias_in, bias_s), (skip_in, skip_s))
+    ]
     get_raw = local(raw_in, rawv)
     get_gain = local(gain_in, gainv.at[0])
     get_x = local(x_in, xv)
@@ -139,6 +143,8 @@
         return value
 
     get_raw.wait()
+    for copy in get_heads:
+        copy.wait()
     speed = jnp.exp(per_head(decay_s, T))
     pre = rawv[...] + per_head(bias_s, T)
     step = jnp.maximum(pre, 0.0) + jnp.log1p(jnp.exp(-jnp.abs(pre)))
@@ -307,6 +313,7 @@
 
     zero = jnp.zeros((8, D), F32)
     gain_sum, skip_sum = tiles(finish, init=(zero, zero))
+
     put_out = local(outv, out_o)
     put_zg = local(zgv, zg_o)
     put_out.start()
@@ -487,11 +494,8 @@
 
     small_out.wait()
     small[24:32] = small[0:8] + small[16:24]
-    put_small = [local(small.at[24, pl.ds(0, D)], gain_o)]
-    for k, ref in enumerate((decay_o, bias_o, skip_o)):
-        ref[...] = small[25 + k, 0:H]
-    for copy in put_small:
-        copy.start()
+    put_params = local(small.at[pl.ds(24, 8)], params_o)
+    put_params.start()
     second_end()
 
     @pl.when(early)
@@ -510,12 +514,31 @@
         for k in range(2):
             start_out[k].wait_send()
 
-    for copy in [put_out, put_zg, put_hg, put_sg] + put_small:
+    for copy in (put_out, put_zg, put_hg, put_sg, put_params):
         copy.wait()
     for copy in [b_right, b_left, c_right, c_left, b_on_right, b_on_left, c_on_right, c_on_left] + norm_out:
         copy.wait_send()
 
 
+def place_results(*refs):
+    results, outputs, held, (get_sem, put_sem) = refs[:7], refs[7:17], refs[17:24], refs[24:]
+    out_o, hg_o, zg_o, sg_o, bg_o, cg_o, decay_o, bias_o, skip_o, gain_o = outputs
+    gets = [pltpu.make_async_copy(src, dst, get_sem.at[k]) for k, (src, dst) in enumerate(zip(results, held))]
+    for copy in gets:
+        copy.start()
+    puts = []
+    rows = held[6]
+    for k, ref in enumerate((out_o, hg_o, zg_o, sg_o, bg_o, cg_o, gain_o)):
+        gets[k].wait()
+        copy = pltpu.make_async_copy(rows.at[0] if ref is gain_o else held[k], ref, put_sem.at[k])
+        copy.start()
+        puts.append(copy)
+    for k, ref in enumerate((decay_o, bias_o, skip_o)):
+        ref[...] = rows[1 + k, 0:H]
+    for copy in puts:
+        copy.wait()
+
+
 def shards(*args):
     def f32(*shape):
         return jax.ShapeDtypeStruct(shape, F32)
@@ -526,10 +549,11 @@
     def vb(*shape):
         return pltpu.VMEM(shape, BF)
 
-    anywhere = pl.BlockSpec(memory_space=pl.ANY)
-    scalars = pl.BlockSpec(memory_space=pltpu.SMEM)
+    in_hbm = pl.BlockSpec(memory_space=pltpu.HBM)
+    in_vmem = pl.BlockSpec(memory_space=pltpu.VMEM)
+    scalars = pltpu.SMEM((H,), F32)
     scratch = [
-        vm(T, D), vm(T, D), vm(T, D), vm(H, T), vm(1, D), vm(N, T), vm(N, T),
+        vm(T, D), vm(T, D), vm(T, D), vm(H, T), vm(1, D), scalars, scalars, scalars, vm(N, T), vm(N, T),
         vm(T, D), vm(T, D), vm(T, D), vm(T, D), vm(T, D), vm(T, D),
         vb(T, D), vb(T, D), vb(Q, D), vb(Q, D), vb(T, D), vb(T, D),
         vb(N, T), vb(N, T), vb(N, T), vb(N, T), vb(T, N), vb(T, N), vb(T, N), vb(T, N),
@@ -539,24 +563,36 @@
         vb(2, N, 256), vb(2, N, 256), vb(2, N, 256), vb(2, N, 256),
         vm(T, D), vm(T, D), vm(N, T), vm(N, T), vm(3 * W, T), vm(3 * W, T), vm(32, D),
         vm(T, D), vm(T, D), vm(T, D), vm(H, T),
-        pltpu.SemaphoreType.DMA((24,)),
+        pltpu.SemaphoreType.DMA((19,)),
         pltpu.SemaphoreType.DMA((28,)),
         pltpu.SemaphoreType.DMA((28,)),
     ]
+    results = pl.pallas_call(
+        body,
+        out_shape=[f32(T, D), f32(T, D), f32(T, D), f32(H, T), f32(W, T), f32(W, T), f32(8, D)],
+        in_specs=[in_hbm] * 10,
+        out_specs=[in_hbm] * 7,
+        scratch_shapes=scratch,
+        compiler_params=pltpu.CompilerParams(
+            collective_id=0, has_side_effects=True, vmem_limit_bytes=64 * 1024 * 1024
+        ),
+        name="layer",
+    )(*args)
     return pl.pallas_call(
-        body,
+        place_results,
         out_shape=[
             f32(T, D), f32(T, D), f32(T, D), f32(H, T), f32(W, T), f32(W, T),
             f32(H), f32(H), f32(H), f32(D),
         ],
-        in_specs=[anywhere] * 5 + [scalars] * 3 + [anywhere] * 2,
-        out_specs=[anywhere] * 6 + [pl.BlockSpec(memory_space=pltpu.VMEM)] * 3 + [anywhere],
-        scratch_shapes=scratch,
-        compiler_params=pltpu.CompilerParams(
-            collective_id=0, has_side_effects=True, vmem_limit_bytes=48 * 1024 * 1024
-        ),
-        name="layer",
-    )(*args)
+        in_specs=[in_hbm] * 7,
+        out_specs=[in_hbm] * 6 + [in_vmem] * 3 + [in_hbm],
+        scratch_shapes=[
+            vm(T, D), vm(T, D), vm(T, D), vm(H, T), vm(W, T), vm(W, T), vm(8, D),
+            pltpu.SemaphoreType.DMA((7,)), pltpu.SemaphoreType.DMA((7,)),
+        ],
+        compiler_params=pltpu.CompilerParams(vmem_limit_bytes=64 * 1024 * 1024),
+        name="place_results",
+    )(*results)
 
 
 def solution(mesh):

time: 50.7 us -> 38.7 us (0.76)
  local copies, waits for them, and re-layouts: 14.5 us -> 0 us
  Pallas kernels: 35.1 us -> 37.9 us
    unnamed x30 -> x0, local copies, waits for them, and re-layouts: 14.5 us -> none
    pallas_call x0 -> x1, Pallas kernels: none -> 2.86 us  [shards(): pl.pallas_call(place_results, out_shape=[f32(T, D), f32(T, D), f32(T, D),...]
where the time goes in v2:
time: 38.7 us; the launch traced here: 38.5 us
  Pallas kernels  37.9 us (98%)
  between operations  0.65 us (2%)
    pallas_call x1, Pallas kernels, shards(): pl.pallas_call(body, out_shape=[f32(T, D), f32(T, D), f32(T, D), f32(H, T...  35 us
    pallas_call x1, Pallas kernels, shards(): pl.pallas_call(place_results, out_shape=[f32(T, D), f32(T, D), f32(T, D),...  2.86 us

profile of v2, /device:TPU:1, one launch (start us, length us, event | category | flops | bytes accessed | tf_op | source)
XLA Modules:
  0.0 38.5 jit_solution(10581455154486975754)
XLA Ops:
  0.6 35.0 %layer.1 = (f32[256,512]{1,0:T(8,128)}, f32[256,512]{1,0:T(8,128)}, f32[256,512]{1,0:T(8,128)}, f32[8,256]{1,0:T(8,128)}, f32[64,256]{1,0:T(8,128)}, /*index=5*/f32[64,256]{1,0:T(8,128)}, f32[8,512]{1,0:T(8,128)}) custom-call(f32[256,512]{1,0:T(8,128)} %x_in.1, f32[256,512]{1,0:T(8,128)} %z_in.1, f32[8,256]{1,0:T(8,128)} %raw_in.1, f32[64,256]{1,0:T(8,128)} %b_in.1, ...), custom_call_target="tpu_custom_call" | custom-call | tf_op jit(solution)/shard_map/layer/pallas_call | solution.py:570
  35.7 2.9 %place_results.1 = (f32[256,512]{1,0:T(8,128)}, f32[256,512]{1,0:T(8,128)}, f32[256,512]{1,0:T(8,128)}, f32[8,256]{1,0:T(8,128)}, f32[64,256]{1,0:T(8,128)}, /*i...) custom-call(f32[256,512]{1,0:T(8,128)} %get-tuple-element.17.refs_0_, ...), custom_call_target="tpu_custom_call" | custom-call | tf_op jit(solution)/shard_map/place_results/pallas_call | solution.py:581

commit v3 on v2

v3 whole, which is shorter than its diff:
```python
import jax
import jax.numpy as jnp
from jax import lax
from jax.experimental import pallas as pl
from jax.experimental.pallas import tpu as pltpu
from jax.sharding import PartitionSpec as P

MESH = pl.DeviceIdType.MESH
F32 = jnp.float32
BF = jnp.bfloat16
T = 256
Q = 128
N = 256
D = 512
H = 8
W = 64
ROWS = 16
TILES = T // ROWS
GROUP_WIDTH = 2048
EPSILON = 1e-05

NN = (((1,), (0,)), ((), ()))
NT = (((1,), (1,)), ((), ()))


def halves(v):
    hi = v.astype(BF)
    return hi, (v - hi.astype(F32)).astype(BF)


def dot(a, b, dims=NN):
    return lax.dot_general(a, b, dims, preferred_element_type=F32)


def dot3(a, b, dims=NN):
    return dot(a[0], b[0], dims) + (dot(a[0], b[1], dims) + dot(a[1], b[0], dims))


def thirds(v):
    hi = v.astype(BF).astype(F32)
    mid = (v - hi).astype(BF).astype(F32)
    return jnp.concatenate([hi, mid, v - hi - mid, jnp.zeros_like(v)], axis=0)


def sum_thirds(v):
    return v[0:8] + (v[8:16] + v[16:24])


def lanes(v):
    return (v[:, 0:128] + v[:, 128:256]) + (v[:, 256:384] + v[:, 384:512])


def fold(v):
    return v[0:8] + v[8:16]


def tiles(step, count=TILES, init=None):
    def run(i, carry):
        return step(pl.ds(pl.multiple_of(i * ROWS, ROWS), ROWS), carry)

    return lax.fori_loop(0, count, run, 0 if init is None else init)


def iota(shape, dim):
    return lax.broadcasted_iota(jnp.int32, shape, dim)


def body(
    x_in, z_in, raw_in, b_in, c_in, decay_in, bias_in, skip_in, gain_in, og_in,
    out_o, hg_o, zg_o, sg_o, bg_o, cg_o, params_o,
    xv, zv, ogv, rawv, gainv, decay_s, bias_s, skip_s, bv, cv, c1v,
    a1, a2, a5, gate, dgate, ogg,
    vh, vl, kh, kl, wh, wl, ph, pld, qh, ql, eh, el, uh, ul,
    bh, bl, ch, cl, cth, ctl, bth, btl, c1h, c1l, gh, gl, gth, gtl, oh, ol, th, tl, fh, fl,
    state, other, sh, sl, ap, ap_in, aq, aq_in, rows, rows_in,
    yi, yv, gated, carry_v, sumh, suml, norm, cols, cols1, d1, d2, k1, k2, dy, yqh, yql,
    dv, dx, first, second, recv_a, recv_b, small, outv, hgv, zgv, sgv,
    local_sem, send_sem, recv_sem,
):
    dp = lax.axis_index("dp")
    ctx = lax.axis_index("ctx")
    place = lax.rem(dp, 4)
    base = dp - place
    right = base + lax.rem(place + 1, 4)
    left = base + lax.rem(place + 3, 4)
    across = base + lax.rem(place + 2, 4)
    early = ctx == 0
    late = ctx == 1

    used = []

    def local(src, dst):
        copy = pltpu.make_async_copy(src, dst, local_sem.at[len(used)])
        used.append(copy)
        return copy

    sent = []

    def remote(src, dst, device):
        k = len(sent)
        sent.append(k)
        return pltpu.make_async_remote_copy(
            src_ref=src, dst_ref=dst, send_sem=send_sem.at[k], recv_sem=recv_sem.at[k],
            device_id=device, device_id_type=MESH,
        )

    to_right, to_left, to_across, to_core = (right, ctx), (left, ctx), (across, ctx), (dp, 1 - ctx)

    barrier = pltpu.get_barrier_semaphore()
    for device in (to_right, to_left, to_across, to_core):
        pl.semaphore_signal(barrier, inc=1, device_id=device, device_id_type=MESH)

    get_heads = [
        local(ref, row)
        for ref, row in ((decay_in, decay_s), (bias_in, bias_s), (skip_in, skip_s))
    ]
    get_raw = local(raw_in, rawv)
    get_gain = local(gain_in, gainv.at[0])
    get_x = local(x_in, xv)
    get_z = local(z_in, zv)
    get_og = local(og_in, ogv)
    get_b = local(b_in, bv.at[pl.ds(0, W)])
    get_c = local(c_in, cv.at[pl.ds(0, W)])
    for copy in used:
        copy.start()
    pl.semaphore_wait(barrier, 4)

    half = W // 2

    def gather(mine, group):
        ahead = [
            remote(mine.at[pl.ds(0, half)], group.at[pl.ds(W, half)], to_right),
            remote(mine.at[pl.ds(half, half)], group.at[pl.ds(2 * W + half, half)], to_left),
        ]
        after = [
            remote(mine.at[pl.ds(half, half)], group.at[pl.ds(W + half, half)], to_right),
            remote(mine.at[pl.ds(0, half)], group.at[pl.ds(2 * W, half)], to_left),
        ]
        onward = [
            remote(group.at[pl.ds(W, half)], group.at[pl.ds(3 * W, half)], to_right),
            remote(group.at[pl.ds(2 * W + half, half)], group.at[pl.ds(3 * W + half, half)], to_left),
        ]
        return ahead, after, onward

    b_ahead, b_after, b_onward = gather(b_in, bv)
    c_ahead, c_after, c_onward = gather(c_in, cv)
    for copy in b_ahead + b_after + c_ahead + c_after:
        copy.start()

    def per_head(ref, width):
        row = iota((H, width), 0)
        value = jnp.full((H, width), ref[0], F32)
        for h in range(1, H):
            value = jnp.where(row == h, ref[h], value)
        return value

    get_raw.wait()
    for copy in get_heads:
        copy.wait()
    speed = jnp.exp(per_head(decay_s, T))
    pre = rawv[...] + per_head(bias_s, T)
    step = jnp.maximum(pre, 0.0) + jnp.log1p(jnp.exp(-jnp.abs(pre)))
    rate = -speed * step
    src, dst = iota((T, T), 0), iota((T, T), 1)
    upto = jnp.where((src <= dst) & (src // Q == dst // Q), 1.0, 0.0).astype(BF)
    run = sum_thirds(dot(thirds(rate).astype(BF), upto))
    total0 = run[:, Q - 1:Q]
    total1 = run[:, T - 1:T]
    position = iota((H, T), 1)
    block1 = position >= Q
    centre = 0.5 * jnp.where(block1, total1, total0)
    scale1 = jnp.exp(run - centre)
    scale2 = step * jnp.exp(centre - run)
    since_start = jnp.where(block1, run + total0, run)
    to_end = jnp.where(block1, total1 - run, total0 - run + total1)
    scale5 = jnp.where(early, step, 1.0) * jnp.exp(jnp.where(early, to_end, since_start))
    stacked = jnp.concatenate(
        [thirds(scale1), thirds(scale2), thirds(scale5), jnp.zeros((32, T), F32)], axis=0
    ).T.astype(BF)
    row, col = iota((128, D), 0), iota((128, D), 1)
    same = (row % 8 == col // W) & (row % 32 < 24)
    for k, ref in enumerate((a1, a2, a5)):
        spread = jnp.where(same & (row // 32 == k), 1.0, 0.0).astype(BF)
        ref[...] = dot(stacked, spread)
    own = iota((H, D), 0) == iota((H, D), 1) // W
    kappa = jnp.sum(
        jnp.where(own, jnp.exp(0.5 * (total0 + total1)), 0.0), axis=0, keepdims=True
    )
    skip_row = jnp.sum(jnp.where(own, per_head(skip_s, D), 0.0), axis=0, keepdims=True)

    for ahead, onward in ((b_ahead, b_onward), (c_ahead, c_onward)):
        for came, goes in zip(ahead, onward):
            came.wait_recv()
            goes.start()

    get_gain.wait()
    get_x.wait()
    get_z.wait()
    get_og.wait()

    def prepare(r, carry):
        z = zv[r]
        sig = 1.0 / (1.0 + jnp.exp(-z))
        g = z * sig
        gate[r] = g
        dgate[r] = sig * (1.0 + z * (1.0 - sig))
        scaled = ogv[r] * gainv[...]
        ogg[r] = scaled
        x = xv[r]
        p = scaled * g
        vh[r], vl[r] = halves(a2[r] * x)
        ph[r], pld[r] = halves(a1[r] * p)
        w = a5[r] * jnp.where(early, x, p)
        ap[r] = w
        wh[r], wl[r] = halves(w)
        return carry

    tiles(prepare)

    ap_out = remote(ap, ap_in, to_core)

    @pl.when(late)
    def _():
        ap_out.start()

    def prepare0(r, carry):
        kh[r], kl[r] = halves((a2[r] * xv[r]) * kappa)
        return carry

    tiles(prepare0, TILES // 2)

    state_out = [remote(state.at[k], other.at[k], to_core) for k in range(4)]

    def end_state(k):
        part = slice(k * W, (k + 1) * W)
        state[k] = dot3((bh[part], bl[part]), (wh[...], wl[...]))
        state_out[k].start()

    get_b.wait()
    for copy in b_ahead:
        copy.wait_send()
    bh[0:W], bl[0:W] = halves(bv[0:W])

    @pl.when(early)
    def _():
        end_state(0)

    def score_grad(out, far, near):
        out[0:Q, 0:Q] = dot3((vh[0:Q], vl[0:Q]), (far[0:Q], near[0:Q]), NT)
        out[0:Q, Q:T] = dot3((kh[...], kl[...]), (far[Q:T], near[Q:T]), NT)
        out[Q:T, Q:T] = dot3((vh[Q:T], vl[Q:T]), (far[Q:T], near[Q:T]), NT)
        out[Q:T, 0:Q] = jnp.zeros((Q, Q), F32)

    score_grad(d1, ph, pld)
    for copy in b_after:
        copy.wait_recv()
    bh[W:3 * W], bl[W:3 * W] = halves(bv[W:3 * W])

    @pl.when(early)
    def _():
        end_state(1)
        end_state(2)

    for copy in b_onward:
        copy.wait_recv()
    bh[3 * W:N], bl[3 * W:N] = halves(bv[3 * W:N])

    @pl.when(early)
    def _():
        end_state(3)

    get_c.wait()
    for copy in c_after:
        copy.wait_recv()
    cth[:, 0:128], ctl[:, 0:128] = halves(cv[0:128].T)
    for copy in c_onward:
        copy.wait_recv()
    cth[:, 128:256], ctl[:, 128:256] = halves(cv[128:256].T)
    c_out = remote(cv, c1v, to_core)

    @pl.when(late)
    def _():
        c_out.start()

    low = src >= dst
    high = src <= dst
    g0 = dot3((cth[0:Q], ctl[0:Q]), (bh[:, 0:Q], bl[:, 0:Q]))
    g1 = dot3((cth[Q:T], ctl[Q:T]), (bh[...], bl[...]))
    gh[0:Q, 0:Q], gl[0:Q, 0:Q] = halves(jnp.where(low[0:Q, 0:Q], g0, 0.0))
    gh[Q:T], gl[Q:T] = halves(jnp.where(low[Q:T], g1, 0.0))
    for k in range(2):
        part = pl.ds(k * 256, 256)
        yi[0:Q, part] = dot3((gh[0:Q, 0:Q], gl[0:Q, 0:Q]), (vh[0:Q, part], vl[0:Q, part]))
        yi[Q:T, part] = dot3(
            (gh[Q:T], gl[Q:T]),
            (
                jnp.concatenate([kh[:, part], vh[Q:T, part]], axis=0),
                jnp.concatenate([kl[:, part], vl[Q:T, part]], axis=0),
            ),
        )

    def mix(r, y):
        yv[r] = y
        mixed = y + skip_row * xv[r]
        g = mixed * gate[r]
        gated[r] = g
        sumh[r, 0:128], suml[r, 0:128] = halves(lanes(g * g))
        sumh[r, 128:256], suml[r, 128:256] = halves(lanes(g * ogg[r]))
        q = g * gate[r]
        qh[r], ql[r] = halves(a1[r] * q)
        return q

    aq_out = remote(aq, aq_in, to_core)

    @pl.when(early)
    def _():
        def go(r, carry):
            mix(r, a1[r] * yi[r])
            return carry

        tiles(go)

    @pl.when(late)
    def _():
        for k in range(4):
            state_out[k].wait_recv()
            sh[k * W:(k + 1) * W], sl[k * W:(k + 1) * W] = halves(other[k])
        for k in range(2):
            part = pl.ds(k * 256, 256)
            carry_v[:, part] = dot3((cth[...], ctl[...]), (sh[:, part], sl[:, part]))

        def go(r, carry):
            w = a5[r] * mix(r, a1[r] * yi[r] + a5[r] * carry_v[r])
            aq[r] = w
            eh[r], el[r] = halves(w)
            return carry

        tiles(go)
        aq_out.start()

    pick = jnp.where(iota((H, 256), 0) == iota((H, 256), 1) // 128, 1.0, 0.0).astype(BF)
    norm[0] = dot(pick, sumh[...], NT) + dot(pick, suml[...], NT)
    norm_out = [
        remote(norm.at[0], norm.at[1 + k], device)
        for k, device in enumerate((to_across, to_right, to_left))
    ]
    for copy in norm_out:
        copy.start()

    score_grad(d2, qh, ql)
    ch[...], cl[...] = halves(cv[...])

    @pl.when(early)
    def _():
        ap_out.wait_recv()
        fh[...], fl[...] = halves(ap_in[...])
        k1[...] = dot3((wh[...], wl[...]), (fh[...], fl[...]), NT)
        bth[...], btl[...] = halves(bv[...].T)
        c_out.wait_recv()
        c1h[...], c1l[...] = halves(c1v[...])

    @pl.when(late)
    def _():
        k1[...] = dot3((sh[...], sl[...]), (wh[...], wl[...]), NT)
        k2[...] = dot3((sh[...], sl[...]), (eh[...], el[...]), NT)

    for copy in norm_out:
        copy.wait_recv()
    sums = (norm[0] + norm[1]) + (norm[2] + norm[3])
    inverse = lax.rsqrt(sums[0:1] * (1.0 / GROUP_WIDTH) + EPSILON)
    slope = inverse * inverse * inverse * sums[1:2] * (1.0 / GROUP_WIDTH)
    rows[...] = jnp.where(iota((8, T), 0) == 0, inverse, slope)
    rows_out = remote(rows, rows_in, to_core)

    @pl.when(late)
    def _():
        rows_out.start()

    full = jnp.where(high, inverse * d1[...] - slope * d2[...], 0.0)
    th[...], tl[...] = halves(full)

    def c_part():
        return dot3((bh[...], bl[...]), (th[...], tl[...]))

    def b_part():
        return dot3((ch[...], cl[...]), (th[...], tl[...]), NT)

    def scatter(parts, landing):
        return [
            remote(parts.at[pl.ds(k * W, W)], landing.at[pl.ds(j * W, W)], device)
            for j, (k, device) in enumerate(((3, to_across), (2, to_right), (1, to_left)))
        ]

    first_out = scatter(first, recv_a)
    second_out = scatter(second, recv_b)

    @pl.when(early)
    def _():
        first[...] = c_part()
        for copy in first_out:
            copy.start()
        second[...] = b_part()
        aq_out.wait_recv()
        oh[...], ol[...] = halves(aq_in[...])
        k2[...] = dot3((wh[...], wl[...]), (oh[...], ol[...]), NT)
        rows_out.wait_recv()
        gth[...], gtl[...] = halves(rows_in[0:1] * k1[...] - rows_in[1:2] * k2[...])
        second[...] += dot3((c1h[...], c1l[...]), (gth[...], gtl[...]), NT)
        for copy in second_out:
            copy.start()

    @pl.when(late)
    def _():
        first[...] = b_part()
        for copy in first_out:
            copy.start()
        second[...] = c_part() + (inverse * k1[...] - slope * k2[...])
        for copy in second_out:
            copy.start()

    lead = iota((128, T), 0)
    cols[...] = jnp.where(lead == 0, inverse, jnp.where(lead == 1, slope, 0.0)).T

    def finish(r, carry):
        gain_sum, skip_sum = carry
        inv = cols[r, 0:1]
        k = cols[r, 1:2]
        g = gated[r]
        x = xv[r]
        y = yv[r]
        normed = g * inv
        outv[r] = normed * gainv[...]
        grad = ogg[r] * inv - g * k
        zgv[r] = grad * (y + skip_row * x) * dgate[r]
        d = grad * gate[r]
        dy[r] = d
        uh[r], ul[r] = halves(a1[r] * d)
        yqh[r], yql[r] = halves(d * y)
        return gain_sum + fold(ogv[r] * normed), skip_sum + fold(d * x)

    zero = jnp.zeros((8, D), F32)
    gain_sum, skip_sum = tiles(finish, init=(zero, zero))
    put_out = local(outv, out_o)
    put_zg = local(zgv, zg_o)
    put_out.start()
    put_zg.start()

    def turned(top, bottom):
        return (gh[top, bottom].astype(F32).T.astype(BF), gl[top, bottom].astype(F32).T.astype(BF))

    lo, hi = slice(0, Q), slice(Q, T)
    g00, g10, g11 = turned(lo, lo), turned(hi, lo), turned(hi, hi)
    for k in range(2):
        part = pl.ds(k * 256, 256)
        dv[0:Q, part] = dot3(g00, (uh[0:Q, part], ul[0:Q, part])) + kappa[
            :, k * 256:(k + 1) * 256
        ] * dot3(g10, (uh[Q:T, part], ul[Q:T, part]))
        dv[Q:T, part] = dot3(g11, (uh[Q:T, part], ul[Q:T, part]))

    small[0:16] = jnp.zeros((16, D), F32)

    def x_grad(r, f):
        hgv[r] = f + skip_row * dy[r]
        uh[r], ul[r] = halves(f * xv[r])

    @pl.when(early)
    def _():
        cols1[...] = jnp.where(lead == 0, rows_in[0:1], jnp.where(lead == 1, rows_in[1:2], 0.0)).T

        def later(r, carry):
            eh[r], el[r] = halves(cols1[r, 0:1] * ap_in[r] - cols1[r, 1:2] * aq_in[r])
            return carry

        tiles(later)
        cross = halves(dot3((bth[...], btl[...]), (c1h[...], c1l[...])))
        for k in range(2):
            part = pl.ds(k * 256, 256)
            dx[:, part] = dot3(cross, (eh[:, part], el[:, part]))

        def go(r, carry):
            tail = a5[r] * dx[r]
            x_grad(r, a2[r] * dv[r] + tail)
            return carry + fold(tail * xv[r])

        small[8:16] = tiles(go, init=zero)

    @pl.when(late)
    def _():
        def go(r, carry):
            x_grad(r, a2[r] * dv[r])
            return carry

        tiles(go)

    put_hg = local(hgv, hg_o)
    put_hg.start()

    heads = jnp.where(own, 1.0, 0.0).astype(BF)
    y_sum = dot(heads, yqh[...], NT) + dot(heads, yql[...], NT)
    x_sum = dot(heads, uh[...], NT) + dot(heads, ul[...], NT)
    from_end = jnp.sum(
        jnp.where(own, jnp.sum(small[8:16], axis=0, keepdims=True), 0.0), axis=1, keepdims=True
    )
    onward = jnp.where(low, 1.0, 0.0).astype(BF)
    rate_grad = sum_thirds(dot(thirds(y_sum - x_sum).astype(BF), onward)) + from_end
    step_grad = (x_sum / step - speed * rate_grad) * (1.0 / (1.0 + jnp.exp(-pre)))
    sgv[...] = step_grad
    put_sg = local(sgv, sg_o)
    put_sg.start()

    def as_row(column):
        hit = iota((H, D), 0) == iota((H, D), 1)
        return jnp.sum(jnp.where(hit, column, 0.0), axis=0, keepdims=True)

    skip_column = jnp.sum(
        jnp.where(own, jnp.sum(skip_sum, axis=0, keepdims=True), 0.0), axis=1, keepdims=True
    )
    small[0:1] = jnp.sum(gain_sum, axis=0, keepdims=True)
    small[1:2] = as_row(jnp.sum(rate_grad * rate, axis=1, keepdims=True))
    small[2:3] = as_row(jnp.sum(step_grad, axis=1, keepdims=True))
    small[3:4] = as_row(skip_column)
    small_out = remote(small.at[pl.ds(0, 8)], small.at[pl.ds(16, 8)], to_core)
    small_out.start()

    def total(parts, landing, copies):
        for copy in copies:
            copy.wait()
        parts[0:W] += landing[0:W] + (landing[W:2 * W] + landing[2 * W:3 * W])

    total(first, recv_a, first_out)
    put_first = [local(first.at[pl.ds(0, W)], o) for o in (cg_o, bg_o)]
    put_second = [local(second.at[pl.ds(0, W)], o) for o in (bg_o, cg_o)]

    @pl.when(early)
    def _():
        put_first[0].start()

    @pl.when(late)
    def _():
        put_first[1].start()

    small_out.wait()
    small[24:32] = small[0:8] + small[16:24]
    put_params = local(small.at[pl.ds(24, 8)], params_o)
    put_params.start()
    total(second, recv_b, second_out)

    @pl.when(early)
    def _():
        put_second[0].start()
        put_first[0].wait()
        put_second[0].wait()
        for copy in state_out:
            copy.wait_send()

    @pl.when(late)
    def _():
        put_second[1].start()
        put_first[1].wait()
        put_second[1].wait()
        for copy in (ap_out, aq_out, c_out, rows_out):
            copy.wait_send()

    for copy in (put_out, put_zg, put_hg, put_sg, put_params):
        copy.wait()
    for copy in b_after + b_onward + c_ahead + c_after + c_onward + norm_out:
        copy.wait_send()


def place_results(*refs):
    results, outputs, held, (get_sem, put_sem) = refs[:7], refs[7:17], refs[17:24], refs[24:]
    out_o, hg_o, zg_o, sg_o, bg_o, cg_o, decay_o, bias_o, skip_o, gain_o = outputs
    gets = [pltpu.make_async_copy(src, dst, get_sem.at[k]) for k, (src, dst) in enumerate(zip(results, held))]
    for copy in gets:
        copy.start()
    puts = []
    rows = held[6]
    for k, ref in enumerate((out_o, hg_o, zg_o, sg_o, bg_o, cg_o, gain_o)):
        gets[k].wait()
        copy = pltpu.make_async_copy(rows.at[0] if ref is gain_o else held[k], ref, put_sem.at[k])
        copy.start()
        puts.append(copy)
    for k, ref in enumerate((decay_o, bias_o, skip_o)):
        ref[...] = rows[1 + k, 0:H]
    for copy in puts:
        copy.wait()


def shards(*args):
    def f32(*shape):
        return jax.ShapeDtypeStruct(shape, F32)

    def vm(*shape):
        return pltpu.VMEM(shape, F32)

    def vb(*shape):
        return pltpu.VMEM(shape, BF)

    in_hbm = pl.BlockSpec(memory_space=pltpu.HBM)
    in_vmem = pl.BlockSpec(memory_space=pltpu.VMEM)
    scalars = pltpu.SMEM((H,), F32)
    wide, narrow = vm(T, D), vb(T, D)
    square, thin = vm(T, T), vb(T, T)
    scratch = [wide] * 3 + [vm(H, T), vm(1, D)] + [scalars] * 3 + [square] * 3
    scratch += [wide] * 6
    scratch += [narrow] * 2 + [vb(Q, D)] * 2 + [narrow] * 10
    scratch += [thin] * 14 + [narrow] * 2 + [thin] * 2 + [narrow] * 2
    scratch += [vm(4, W, D)] * 2 + [narrow] * 2 + [wide] * 4 + [vm(8, T)] * 2
    scratch += [wide] * 4 + [thin] * 2 + [vm(4, 8, T), vm(T, 128), vm(T, 128)]
    scratch += [square] * 4 + [wide] + [narrow] * 2
    scratch += [wide] * 2 + [square] * 2 + [vm(3 * W, T)] * 2 + [vm(32, D)] + [wide] * 3 + [vm(H, T)]
    scratch += [
        pltpu.SemaphoreType.DMA((19,)),
        pltpu.SemaphoreType.DMA((31,)),
        pltpu.SemaphoreType.DMA((31,)),
    ]
    results = pl.pallas_call(
        body,
        out_shape=[f32(T, D), f32(T, D), f32(T, D), f32(H, T), f32(W, T), f32(W, T), f32(8, D)],
        in_specs=[in_hbm] * 10,
        out_specs=[in_hbm] * 7,
        scratch_shapes=scratch,
        compiler_params=pltpu.CompilerParams(
            collective_id=0, has_side_effects=True, vmem_limit_bytes=64 * 1024 * 1024
        ),
        name="layer",
    )(*args)
    return pl.pallas_call(
        place_results,
        out_shape=[
            f32(T, D), f32(T, D), f32(T, D), f32(H, T), f32(W, T), f32(W, T),
            f32(H), f32(H), f32(H), f32(D),
        ],
        in_specs=[in_hbm] * 7,
        out_specs=[in_hbm] * 6 + [in_vmem] * 3 + [in_hbm],
        scratch_shapes=[
            vm(T, D), vm(T, D), vm(T, D), vm(H, T), vm(W, T), vm(W, T), vm(8, D),
            pltpu.SemaphoreType.DMA((7,)), pltpu.SemaphoreType.DMA((7,)),
        ],
        compiler_params=pltpu.CompilerParams(vmem_limit_bytes=64 * 1024 * 1024),
        name="place_results",
    )(*results)


def solution(mesh):
    rows, cols = P("ctx", "dp"), P("dp", "ctx")
    heads = P("dp")
    return jax.shard_map(
        shards,
        mesh=mesh,
        in_specs=(rows, rows, cols, cols, cols, heads, heads, heads, heads, rows),
        out_specs=(rows, rows, rows, cols, cols, cols, heads, heads, heads, heads),
        check_vma=False,
    )
```

time: 38.7 us -> 34.7 us (0.90)
  Pallas kernels: 37.9 us -> 33.9 us
    pallas_call x1, Pallas kernels: 35 us -> 31 us  [shards(): pl.pallas_call(body, out_shape=[f32(T, D), f32(T, D), f32(T, D), f32(H, T...]
where the time goes in v3:
time: 34.7 us; the launch traced here: 34.5 us
  Pallas kernels  33.9 us (98%)
  between operations  0.65 us (2%)
    pallas_call x1, Pallas kernels, shards(): pl.pallas_call(body, out_shape=[f32(T, D), f32(T, D), f32(T, D), f32(H, T...  31 us
    pallas_call x1, Pallas kernels, shards(): pl.pallas_call(place_results, out_shape=[f32(T, D), f32(T, D), f32(T, D),...  2.86 us

profile of v3, /device:TPU:1, one launch (start us, length us, event | category | flops | bytes accessed | tf_op | source)
XLA Modules:
  0.0 34.5 jit_solution(243071258599896878)
XLA Ops:
  0.6 31.0 %layer.1 = (f32[256,512]{1,0:T(8,128)}, f32[256,512]{1,0:T(8,128)}, f32[256,512]{1,0:T(8,128)}, f32[8,256]{1,0:T(8,128)}, f32[64,256]{1,0:T(8,128)}, /*index=5*/f32[64,256]{1,0:T(8,128)}, f32[8,512]{1,0:T(8,128)}) custom-call(f32[256,512]{1,0:T(8,128)} %x_in.1, f32[256,512]{1,0:T(8,128)} %z_in.1, f32[8,256]{1,0:T(8,128)} %raw_in.1, f32[64,256]{1,0:T(8,128)} %b_in.1, ...), custom_call_target="tpu_custom_call" | custom-call | tf_op jit(solution)/shard_map/layer/pallas_call | solution.py:617
  31.6 2.9 %place_results.1 = (f32[256,512]{1,0:T(8,128)}, f32[256,512]{1,0:T(8,128)}, f32[256,512]{1,0:T(8,128)}, f32[8,256]{1,0:T(8,128)}, f32[64,256]{1,0:T(8,128)}, /*i...) custom-call(f32[256,512]{1,0:T(8,128)} %get-tuple-element.17.refs_0_, ...), custom_call_target="tpu_custom_call" | custom-call | tf_op jit(solution)/shard_map/place_results/pallas_call | solution.py:628

commit v4 on v3

--- a/solution.py
+++ b/solution.py
@@ -67,14 +67,14 @@
 
 def body(
     x_in, z_in, raw_in, b_in, c_in, decay_in, bias_in, skip_in, gain_in, og_in,
-    out_o, hg_o, zg_o, sg_o, bg_o, cg_o, params_o,
+    outv, hgv, zgv, sgv, bgv, cgv, params,
     xv, zv, ogv, rawv, gainv, decay_s, bias_s, skip_s, bv, cv, c1v,
     a1, a2, a5, gate, dgate, ogg,
     vh, vl, kh, kl, wh, wl, ph, pld, qh, ql, eh, el, uh, ul,
     bh, bl, ch, cl, cth, ctl, bth, btl, c1h, c1l, gh, gl, gth, gtl, oh, ol, th, tl, fh, fl,
     state, other, sh, sl, ap, ap_in, aq, aq_in, rows, rows_in,
     yi, yv, gated, carry_v, sumh, suml, norm, cols, cols1, d1, d2, k1, k2, dy, yqh, yql,
-    dv, dx, first, second, recv_a, recv_b, small, outv, hgv, zgv, sgv,
+    dv, dx, first, second, recv_a, recv_b, small,
     local_sem, send_sem, recv_sem,
 ):
     dp = lax.axis_index("dp")
@@ -123,6 +123,24 @@
     get_c = local(c_in, cv.at[pl.ds(0, W)])
     for copy in used:
         copy.start()
+    def per_head(ref, width):
+        row = iota((H, width), 0)
+        value = jnp.full((H, width), ref[0], F32)
+        for h in range(1, H):
+            value = jnp.where(row == h, ref[h], value)
+        return value
+
+    get_raw.wait()
+    for copy in get_heads:
+        copy.wait()
+    speed = jnp.exp(per_head(decay_s, T))
+    pre = rawv[...] + per_head(bias_s, T)
+    step = jnp.maximum(pre, 0.0) + jnp.log1p(jnp.exp(-jnp.abs(pre)))
+    rate = -speed * step
+    src, dst = iota((T, T), 0), iota((T, T), 1)
+    upto = jnp.where((src <= dst) & (src // Q == dst // Q), 1.0, 0.0).astype(BF)
+    run = sum_thirds(dot(thirds(rate).astype(BF), upto))
+
     pl.semaphore_wait(barrier, 4)
 
     half = W // 2
@@ -144,26 +162,9 @@
 
     b_ahead, b_after, b_onward = gather(b_in, bv)
     c_ahead, c_after, c_onward = gather(c_in, cv)
-    for copy in b_ahead + b_after + c_ahead + c_after:
+    for copy in b_ahead + c_ahead:
         copy.start()
 
-    def per_head(ref, width):
-        row = iota((H, width), 0)
-        value = jnp.full((H, width), ref[0], F32)
-        for h in range(1, H):
-            value = jnp.where(row == h, ref[h], value)
-        return value
-
-    get_raw.wait()
-    for copy in get_heads:
-        copy.wait()
-    speed = jnp.exp(per_head(decay_s, T))
-    pre = rawv[...] + per_head(bias_s, T)
-    step = jnp.maximum(pre, 0.0) + jnp.log1p(jnp.exp(-jnp.abs(pre)))
-    rate = -speed * step
-    src, dst = iota((T, T), 0), iota((T, T), 1)
-    upto = jnp.where((src <= dst) & (src // Q == dst // Q), 1.0, 0.0).astype(BF)
-    run = sum_thirds(dot(thirds(rate).astype(BF), upto))
     total0 = run[:, Q - 1:Q]
     total1 = run[:, T - 1:T]
     position = iota((H, T), 1)
@@ -182,6 +183,9 @@
     for k, ref in enumerate((a1, a2, a5)):
         spread = jnp.where(same & (row // 32 == k), 1.0, 0.0).astype(BF)
         ref[...] = dot(stacked, spread)
+    for copy in b_after + c_after:
+        copy.start()
+
     own = iota((H, D), 0) == iota((H, D), 1) // W
     kappa = jnp.sum(
         jnp.where(own, jnp.exp(0.5 * (total0 + total1)), 0.0), axis=0, keepdims=True
@@ -237,8 +241,6 @@
         state_out[k].start()
 
     get_b.wait()
-    for copy in b_ahead:
-        copy.wait_send()
     bh[0:W], bl[0:W] = halves(bv[0:W])
 
     @pl.when(early)
@@ -386,19 +388,39 @@
         return dot3((ch[...], cl[...]), (th[...], tl[...]), NT)
 
     def scatter(parts, landing):
-        return [
-            remote(parts.at[pl.ds(k * W, W)], landing.at[pl.ds(j * W, W)], device)
-            for j, (k, device) in enumerate(((3, to_across), (2, to_right), (1, to_left)))
+        far = [
+            remote(parts.at[pl.ds(3 * W, half)], landing.at[pl.ds(0, half)], to_right),
+            remote(parts.at[pl.ds(3 * W + half, half)], landing.at[pl.ds(half, half)], to_left),
         ]
-
-    first_out = scatter(first, recv_a)
-    second_out = scatter(second, recv_b)
+        near = [
+            remote(parts.at[pl.ds(2 * W + half, half)], landing.at[pl.ds(W + half, half)], to_right),
+            remote(parts.at[pl.ds(W, half)], landing.at[pl.ds(2 * W, half)], to_left),
+        ]
+        total = [
+            remote(parts.at[pl.ds(2 * W, half)], landing.at[pl.ds(W, half)], to_right),
+            remote(parts.at[pl.ds(W + half, half)], landing.at[pl.ds(2 * W + half, half)], to_left),
+        ]
+        return far, near, total
+
+    def relay(parts, landing, far, total):
+        far[0].wait_recv()
+        parts[2 * W:2 * W + half] += landing[0:half]
+        total[0].start()
+        far[1].wait_recv()
+        parts[W + half:2 * W] += landing[half:W]
+        total[1].start()
+
+    first_far, first_near, first_total = scatter(first, recv_a)
+    second_far, second_near, second_total = scatter(second, recv_b)
+
+    def begin(copies):
+        for copy in copies:
+            copy.start()
 
     @pl.when(early)
     def _():
         first[...] = c_part()
-        for copy in first_out:
-            copy.start()
+        begin(first_far)
         second[...] = b_part()
         aq_out.wait_recv()
         oh[...], ol[...] = halves(aq_in[...])
@@ -406,17 +428,16 @@
         rows_out.wait_recv()
         gth[...], gtl[...] = halves(rows_in[0:1] * k1[...] - rows_in[1:2] * k2[...])
         second[...] += dot3((c1h[...], c1l[...]), (gth[...], gtl[...]), NT)
-        for copy in second_out:
-            copy.start()
+        begin(second_far)
 
     @pl.when(late)
     def _():
         first[...] = b_part()
-        for copy in first_out:
-            copy.start()
+        begin(first_far)
         second[...] = c_part() + (inverse * k1[...] - slope * k2[...])
-        for copy in second_out:
-            copy.start()
+        begin(second_far)
+
+    begin(first_near)
 
     lead = iota((128, T), 0)
     cols[...] = jnp.where(lead == 0, inverse, jnp.where(lead == 1, slope, 0.0)).T
@@ -440,10 +461,8 @@
 
     zero = jnp.zeros((8, D), F32)
     gain_sum, skip_sum = tiles(finish, init=(zero, zero))
-    put_out = local(outv, out_o)
-    put_zg = local(zgv, zg_o)
-    put_out.start()
-    put_zg.start()
+
+    begin(second_near)
 
     def turned(top, bottom):
         return (gh[top, bottom].astype(F32).T.astype(BF), gl[top, bottom].astype(F32).T.astype(BF))
@@ -457,6 +476,8 @@
         ] * dot3(g10, (uh[Q:T, part], ul[Q:T, part]))
         dv[Q:T, part] = dot3(g11, (uh[Q:T, part], ul[Q:T, part]))
 
+    relay(first, recv_a, first_far, first_total)
+    relay(second, recv_b, second_far, second_total)
     small[0:16] = jnp.zeros((16, D), F32)
 
     def x_grad(r, f):
@@ -492,8 +513,6 @@
 
         tiles(go)
 
-    put_hg = local(hgv, hg_o)
-    put_hg.start()
 
     heads = jnp.where(own, 1.0, 0.0).astype(BF)
     y_sum = dot(heads, yqh[...], NT) + dot(heads, yql[...], NT)
@@ -505,8 +524,6 @@
     rate_grad = sum_thirds(dot(thirds(y_sum - x_sum).astype(BF), onward)) + from_end
     step_grad = (x_sum / step - speed * rate_grad) * (1.0 / (1.0 + jnp.exp(-pre)))
     sgv[...] = step_grad
-    put_sg = local(sgv, sg_o)
-    put_sg.start()
 
     def as_row(column):
         hit = iota((H, D), 0) == iota((H, D), 1)
@@ -522,67 +539,48 @@
     small_out = remote(small.at[pl.ds(0, 8)], small.at[pl.ds(16, 8)], to_core)
     small_out.start()
 
-    def total(parts, landing, copies):
-        for copy in copies:
-            copy.wait()
-        parts[0:W] += landing[0:W] + (landing[W:2 * W] + landing[2 * W:3 * W])
-
-    total(first, recv_a, first_out)
-    put_first = [local(first.at[pl.ds(0, W)], o) for o in (cg_o, bg_o)]
-    put_second = [local(second.at[pl.ds(0, W)], o) for o in (bg_o, cg_o)]
-
-    @pl.when(early)
-    def _():
-        put_first[0].start()
-
-    @pl.when(late)
-    def _():
-        put_first[1].start()
-
-    small_out.wait()
-    small[24:32] = small[0:8] + small[16:24]
-    put_params = local(small.at[pl.ds(24, 8)], params_o)
-    put_params.start()
-    total(second, recv_b, second_out)
-
-    @pl.when(early)
-    def _():
-        put_second[0].start()
-        put_first[0].wait()
-        put_second[0].wait()
+    for copy in small_out, *first_near, *first_total:
+        copy.wait_recv()
+    params[...] = small[0:8] + small[16:24]
+    first_sum = first[0:W] + (recv_a[W:2 * W] + recv_a[2 * W:3 * W])
+    for copy in second_near + second_total:
+        copy.wait_recv()
+    second_sum = second[0:W] + (recv_b[W:2 * W] + recv_b[2 * W:3 * W])
+
+    @pl.when(early)
+    def _():
+        cgv[...] = first_sum
+        bgv[...] = second_sum
         for copy in state_out:
             copy.wait_send()
 
     @pl.when(late)
     def _():
-        put_second[1].start()
-        put_first[1].wait()
-        put_second[1].wait()
+        bgv[...] = first_sum
+        cgv[...] = second_sum
         for copy in (ap_out, aq_out, c_out, rows_out):
             copy.wait_send()
 
-    for copy in (put_out, put_zg, put_hg, put_sg, put_params):
-        copy.wait()
-    for copy in b_after + b_onward + c_ahead + c_after + c_onward + norm_out:
+    for copy in b_ahead + b_after + b_onward + c_ahead + c_after + c_onward + norm_out:
         copy.wait_send()
+    for copy in first_far + first_near + first_total + second_far + second_near + second_total:
+        copy.wait_send()
+    small_out.wait_send()
 
 
 def place_results(*refs):
-    results, outputs, held, (get_sem, put_sem) = refs[:7], refs[7:17], refs[17:24], refs[24:]
+    results, outputs, sem = refs[:7], refs[7:17], refs[17]
     out_o, hg_o, zg_o, sg_o, bg_o, cg_o, decay_o, bias_o, skip_o, gain_o = outputs
-    gets = [pltpu.make_async_copy(src, dst, get_sem.at[k]) for k, (src, dst) in enumerate(zip(results, held))]
-    for copy in gets:
+    rows = results[6]
+    copies = [
+        pltpu.make_async_copy(rows.at[0] if ref is gain_o else results[k], ref, sem.at[k])
+        for k, ref in enumerate((out_o, hg_o, zg_o, sg_o, bg_o, cg_o, gain_o))
+    ]
+    for copy in copies:
         copy.start()
-    puts = []
-    rows = held[6]
-    for k, ref in enumerate((out_o, hg_o, zg_o, sg_o, bg_o, cg_o, gain_o)):
-        gets[k].wait()
-        copy = pltpu.make_async_copy(rows.at[0] if ref is gain_o else held[k], ref, put_sem.at[k])
-        copy.start()
-        puts.append(copy)
     for k, ref in enumerate((decay_o, bias_o, skip_o)):
         ref[...] = rows[1 + k, 0:H]
-    for copy in puts:
+    for copy in copies:
         copy.wait()
 
 
@@ -608,20 +606,21 @@
     scratch += [vm(4, W, D)] * 2 + [narrow] * 2 + [wide] * 4 + [vm(8, T)] * 2
     scratch += [wide] * 4 + [thin] * 2 + [vm(4, 8, T), vm(T, 128), vm(T, 128)]
     scratch += [square] * 4 + [wide] + [narrow] * 2
-    scratch += [wide] * 2 + [square] * 2 + [vm(3 * W, T)] * 2 + [vm(32, D)] + [wide] * 3 + [vm(H, T)]
+    scratch += [wide] * 2 + [square] * 2 + [vm(3 * W, T)] * 2 + [vm(32, D)]
     scratch += [
-        pltpu.SemaphoreType.DMA((19,)),
-        pltpu.SemaphoreType.DMA((31,)),
-        pltpu.SemaphoreType.DMA((31,)),
+        pltpu.SemaphoreType.DMA((10,)),
+        pltpu.SemaphoreType.DMA((37,)),
+        pltpu.SemaphoreType.DMA((37,)),
     ]
+    args = [pltpu.with_memory_space_constraint(array, pltpu.HBM) for array in args]
     results = pl.pallas_call(
         body,
         out_shape=[f32(T, D), f32(T, D), f32(T, D), f32(H, T), f32(W, T), f32(W, T), f32(8, D)],
         in_specs=[in_hbm] * 10,
-        out_specs=[in_hbm] * 7,
+        out_specs=[in_vmem] * 7,
         scratch_shapes=scratch,
         compiler_params=pltpu.CompilerParams(
-            collective_id=0, has_side_effects=True, vmem_limit_bytes=64 * 1024 * 1024
+            collective_id=0, has_side_effects=True, vmem_limit_bytes=40 * 1024 * 1024
         ),
         name="layer",
     )(*args)
@@ -631,13 +630,10 @@
             f32(T, D), f32(T, D), f32(T, D), f32(H, T), f32(W, T), f32(W, T),
             f32(H), f32(H), f32(H), f32(D),
         ],
-        in_specs=[in_hbm] * 7,
+        in_specs=[in_vmem] * 7,
         out_specs=[in_hbm] * 6 + [in_vmem] * 3 + [in_hbm],
-        scratch_shapes=[
-            vm(T, D), vm(T, D), vm(T, D), vm(H, T), vm(W, T), vm(W, T), vm(8, D),
-            pltpu.SemaphoreType.DMA((7,)), pltpu.SemaphoreType.DMA((7,)),
-        ],
-        compiler_params=pltpu.CompilerParams(vmem_limit_bytes=64 * 1024 * 1024),
+        scratch_shapes=[pltpu.SemaphoreType.DMA((7,))],
+        compiler_params=pltpu.CompilerParams(vmem_limit_bytes=16 * 1024 * 1024),
         name="place_results",
     )(*results)
 

time: 34.7 us -> 33.3 us (0.960)
  Pallas kernels: 33.9 us -> 32.5 us
    pallas_call x1, Pallas kernels: 2.86 us -> 1.76 us  [shards(): pl.pallas_call(place_results, out_shape=[f32(T, D), f32(T, D), f32(T, D),...]
where the time goes in v4:
time: 33.3 us; the launch traced here: 33.2 us
  Pallas kernels  32.5 us (98%)
  between operations  0.65 us (2%)
    pallas_call x1, Pallas kernels, shards(): pl.pallas_call(body, out_shape=[f32(T, D), f32(T, D), f32(T, D), f32(H, T...  30.8 us
    pallas_call x1, Pallas kernels, shards(): pl.pallas_call(place_results, out_shape=[f32(T, D), f32(T, D), f32(T, D),...  1.76 us

profile of v4, /device:TPU:1, one launch (start us, length us, event | category | flops | bytes accessed | tf_op | source)
XLA Modules:
  0.0 33.2 jit_solution(9820642182564685758)
XLA Ops:
  0.6 30.8 %layer.1 = (f32[256,512]{1,0:T(8,128)S(1)}, f32[256,512]{1,0:T(8,128)S(1)}, f32[256,512]{1,0:T(8,128)S(1)}, f32[8,256]{1,0:T(8,128)S(1)}, f32[64,256]{1,0:T(8,12...) custom-call(f32[256,512]{1,0:T(8,128)} %x_in.1, f32[256,512]{1,0:T(8,128)} %z_in.1, f32[8,256]{1,0:T(8,128)} %raw_in.1, ...), custom_call_target="tpu_custom_call" | custom-call | tf_op jit(solution)/shard_map/layer/pallas_call | solution.py:616
  31.4 1.8 %place_results.1 = (f32[256,512]{1,0:T(8,128)}, f32[256,512]{1,0:T(8,128)}, f32[256,512]{1,0:T(8,128)}, f32[8,256]{1,0:T(8,128)}, f32[64,256]{1,0:T(8,128)}, /*i...) custom-call(f32[256,512]{1,0:T(8,128)S(1)} %get-tuple-element.17.refs_0_, ...), custom_call_target="tpu_custom_call" | custom-call | tf_op jit(solution)/shard_map/place_results/pallas_call | solution.py:627

commit v5 on v4

--- a/solution.py
+++ b/solution.py
@@ -54,9 +54,9 @@
     return v[0:8] + v[8:16]
 
 
-def tiles(step, count=TILES, init=None):
+def tiles(step, count=TILES, init=None, first=0):
     def run(i, carry):
-        return step(pl.ds(pl.multiple_of(i * ROWS, ROWS), ROWS), carry)
+        return step(pl.ds(pl.multiple_of(first + i * ROWS, ROWS), ROWS), carry)
 
     return lax.fori_loop(0, count, run, 0 if init is None else init)
 
@@ -74,7 +74,7 @@
     bh, bl, ch, cl, cth, ctl, bth, btl, c1h, c1l, gh, gl, gth, gtl, oh, ol, th, tl, fh, fl,
     state, other, sh, sl, ap, ap_in, aq, aq_in, rows, rows_in,
     yi, yv, gated, carry_v, sumh, suml, norm, cols, cols1, d1, d2, k1, k2, dy, yqh, yql,
-    dv, dx, first, second, recv_a, recv_b, small,
+    dv, dx, b_part, c_part, recv_b, recv_c, small,
     local_sem, send_sem, recv_sem,
 ):
     dp = lax.axis_index("dp")
@@ -143,27 +143,26 @@
 
     pl.semaphore_wait(barrier, 4)
 
-    half = W // 2
-
-    def gather(mine, group):
-        ahead = [
-            remote(mine.at[pl.ds(0, half)], group.at[pl.ds(W, half)], to_right),
-            remote(mine.at[pl.ds(half, half)], group.at[pl.ds(2 * W + half, half)], to_left),
+    lo, hi = slice(0, Q), slice(Q, T)
+
+    def gather(mine, group, j):
+        part = pl.ds(j * Q, Q)
+        return [
+            remote(mine.at[:, part], group.at[pl.ds(k * W, W), part], device)
+            for k, device in ((3, to_across), (1, to_right), (2, to_left))
         ]
-        after = [
-            remote(mine.at[pl.ds(half, half)], group.at[pl.ds(W + half, half)], to_right),
-            remote(mine.at[pl.ds(0, half)], group.at[pl.ds(2 * W, half)], to_left),
-        ]
-        onward = [
-            remote(group.at[pl.ds(W, half)], group.at[pl.ds(3 * W, half)], to_right),
-            remote(group.at[pl.ds(2 * W + half, half)], group.at[pl.ds(3 * W + half, half)], to_left),
-        ]
-        return ahead, after, onward
-
-    b_ahead, b_after, b_onward = gather(b_in, bv)
-    c_ahead, c_after, c_onward = gather(c_in, cv)
-    for copy in b_ahead + c_ahead:
-        copy.start()
+
+    def begin(copies):
+        for copy in copies:
+            copy.start()
+
+    def arrive(copies):
+        for copy in copies:
+            copy.wait_recv()
+
+    b_copies = [gather(b_in, bv, j) for j in range(2)]
+    c_copies = [gather(c_in, cv, j) for j in range(2)]
+    begin(b_copies[0] + c_copies[0])
 
     total0 = run[:, Q - 1:Q]
     total1 = run[:, T - 1:T]
@@ -183,19 +182,13 @@
     for k, ref in enumerate((a1, a2, a5)):
         spread = jnp.where(same & (row // 32 == k), 1.0, 0.0).astype(BF)
         ref[...] = dot(stacked, spread)
-    for copy in b_after + c_after:
-        copy.start()
+    begin(b_copies[1] + c_copies[1])
 
     own = iota((H, D), 0) == iota((H, D), 1) // W
     kappa = jnp.sum(
         jnp.where(own, jnp.exp(0.5 * (total0 + total1)), 0.0), axis=0, keepdims=True
     )
     skip_row = jnp.sum(jnp.where(own, per_head(skip_s, D), 0.0), axis=0, keepdims=True)
-
-    for ahead, onward in ((b_ahead, b_onward), (c_ahead, c_onward)):
-        for came, goes in zip(ahead, onward):
-            came.wait_recv()
-            goes.start()
 
     get_gain.wait()
     get_x.wait()
@@ -233,73 +226,26 @@
 
     tiles(prepare0, TILES // 2)
 
-    state_out = [remote(state.at[k], other.at[k], to_core) for k in range(4)]
-
-    def end_state(k):
-        part = slice(k * W, (k + 1) * W)
-        state[k] = dot3((bh[part], bl[part]), (wh[...], wl[...]))
-        state_out[k].start()
-
-    get_b.wait()
-    bh[0:W], bl[0:W] = halves(bv[0:W])
-
-    @pl.when(early)
-    def _():
-        end_state(0)
-
     def score_grad(out, far, near):
         out[0:Q, 0:Q] = dot3((vh[0:Q], vl[0:Q]), (far[0:Q], near[0:Q]), NT)
         out[0:Q, Q:T] = dot3((kh[...], kl[...]), (far[Q:T], near[Q:T]), NT)
         out[Q:T, Q:T] = dot3((vh[Q:T], vl[Q:T]), (far[Q:T], near[Q:T]), NT)
-        out[Q:T, 0:Q] = jnp.zeros((Q, Q), F32)
 
     score_grad(d1, ph, pld)
-    for copy in b_after:
-        copy.wait_recv()
-    bh[W:3 * W], bl[W:3 * W] = halves(bv[W:3 * W])
-
-    @pl.when(early)
-    def _():
-        end_state(1)
-        end_state(2)
-
-    for copy in b_onward:
-        copy.wait_recv()
-    bh[3 * W:N], bl[3 * W:N] = halves(bv[3 * W:N])
-
-    @pl.when(early)
-    def _():
-        end_state(3)
-
-    get_c.wait()
-    for copy in c_after:
-        copy.wait_recv()
-    cth[:, 0:128], ctl[:, 0:128] = halves(cv[0:128].T)
-    for copy in c_onward:
-        copy.wait_recv()
-    cth[:, 128:256], ctl[:, 128:256] = halves(cv[128:256].T)
-    c_out = remote(cv, c1v, to_core)
-
-    @pl.when(late)
-    def _():
-        c_out.start()
 
     low = src >= dst
     high = src <= dst
-    g0 = dot3((cth[0:Q], ctl[0:Q]), (bh[:, 0:Q], bl[:, 0:Q]))
-    g1 = dot3((cth[Q:T], ctl[Q:T]), (bh[...], bl[...]))
-    gh[0:Q, 0:Q], gl[0:Q, 0:Q] = halves(jnp.where(low[0:Q, 0:Q], g0, 0.0))
-    gh[Q:T], gl[Q:T] = halves(jnp.where(low[Q:T], g1, 0.0))
+    get_b.wait()
+    get_c.wait()
+    arrive(b_copies[0])
+    bh[:, lo], bl[:, lo] = halves(bv[:, lo])
+    arrive(c_copies[0])
+    cth[lo], ctl[lo] = halves(cv[:, lo].T)
+    g0 = dot3((cth[lo], ctl[lo]), (bh[:, lo], bl[:, lo]))
+    gh[lo, lo], gl[lo, lo] = halves(jnp.where(low[lo, lo], g0, 0.0))
     for k in range(2):
         part = pl.ds(k * 256, 256)
-        yi[0:Q, part] = dot3((gh[0:Q, 0:Q], gl[0:Q, 0:Q]), (vh[0:Q, part], vl[0:Q, part]))
-        yi[Q:T, part] = dot3(
-            (gh[Q:T], gl[Q:T]),
-            (
-                jnp.concatenate([kh[:, part], vh[Q:T, part]], axis=0),
-                jnp.concatenate([kl[:, part], vl[Q:T, part]], axis=0),
-            ),
-        )
+        yi[lo, part] = dot3((gh[lo, lo], gl[lo, lo]), (vh[lo, part], vl[lo, part]))
 
     def mix(r, y):
         yv[r] = y
@@ -312,20 +258,72 @@
         qh[r], ql[r] = halves(a1[r] * q)
         return q
 
-    aq_out = remote(aq, aq_in, to_core)
-
-    @pl.when(early)
-    def _():
+    pick = jnp.where(iota((H, 256), 0) == iota((H, 256), 1) // 128, 1.0, 0.0).astype(BF)
+    norm_out = [
+        [
+            remote(norm.at[j, 0], norm.at[j, 1 + k], device)
+            for k, device in enumerate((to_across, to_right, to_left))
+        ]
+        for j in range(2)
+    ]
+
+    def send_sums(j, block):
+        norm[j, 0] = dot(pick, sumh[block], NT) + dot(pick, suml[block], NT)
+        begin(norm_out[j])
+
+    def mix_early(j, block):
         def go(r, carry):
             mix(r, a1[r] * yi[r])
             return carry
 
-        tiles(go)
+        tiles(go, TILES // 2, first=j * Q)
+        send_sums(j, block)
+
+    @pl.when(early)
+    def _():
+        mix_early(0, lo)
+
+    state_out = [remote(state.at[k], other.at[k], to_core) for k in range(4)]
+    arrive(b_copies[1])
+    bh[:, hi], bl[:, hi] = halves(bv[:, hi])
+
+    @pl.when(early)
+    def _():
+        for k in range(4):
+            part = slice(k * W, (k + 1) * W)
+            state[k] = dot3((bh[part], bl[part]), (wh[...], wl[...]))
+            state_out[k].start()
+
+    arrive(c_copies[1])
+    cth[hi], ctl[hi] = halves(cv[:, hi].T)
+    c_out = remote(cv, c1v, to_core)
 
     @pl.when(late)
     def _():
+        c_out.start()
+
+    g1 = dot3((cth[hi], ctl[hi]), (bh[...], bl[...]))
+    gh[hi], gl[hi] = halves(jnp.where(low[hi], g1, 0.0))
+    for k in range(2):
+        part = pl.ds(k * 256, 256)
+        yi[hi, part] = dot3(
+            (gh[hi], gl[hi]),
+            (
+                jnp.concatenate([kh[:, part], vh[hi, part]], axis=0),
+                jnp.concatenate([kl[:, part], vl[hi, part]], axis=0),
+            ),
+        )
+
+    aq_out = remote(aq, aq_in, to_core)
+
+    @pl.when(early)
+    def _():
+        mix_early(1, hi)
+
+    @pl.when(late)
+    def _():
+        arrive(state_out)
         for k in range(4):
-            state_out[k].wait_recv()
             sh[k * W:(k + 1) * W], sl[k * W:(k + 1) * W] = halves(other[k])
         for k in range(2):
             part = pl.ds(k * 256, 256)
@@ -337,17 +335,11 @@
             eh[r], el[r] = halves(w)
             return carry
 
-        tiles(go)
+        tiles(go, TILES // 2)
+        send_sums(0, lo)
+        tiles(go, TILES // 2, first=Q)
+        send_sums(1, hi)
         aq_out.start()
-
-    pick = jnp.where(iota((H, 256), 0) == iota((H, 256), 1) // 128, 1.0, 0.0).astype(BF)
-    norm[0] = dot(pick, sumh[...], NT) + dot(pick, suml[...], NT)
-    norm_out = [
-        remote(norm.at[0], norm.at[1 + k], device)
-        for k, device in enumerate((to_across, to_right, to_left))
-    ]
-    for copy in norm_out:
-        copy.start()
 
     score_grad(d2, qh, ql)
     ch[...], cl[...] = halves(cv[...])
@@ -366,81 +358,64 @@
         k1[...] = dot3((sh[...], sl[...]), (wh[...], wl[...]), NT)
         k2[...] = dot3((sh[...], sl[...]), (eh[...], el[...]), NT)
 
-    for copy in norm_out:
-        copy.wait_recv()
-    sums = (norm[0] + norm[1]) + (norm[2] + norm[3])
-    inverse = lax.rsqrt(sums[0:1] * (1.0 / GROUP_WIDTH) + EPSILON)
-    slope = inverse * inverse * inverse * sums[1:2] * (1.0 / GROUP_WIDTH)
-    rows[...] = jnp.where(iota((8, T), 0) == 0, inverse, slope)
+    def factors(j, block):
+        arrive(norm_out[j])
+        sums = (norm[j, 0] + norm[j, 1]) + (norm[j, 2] + norm[j, 3])
+        inv = lax.rsqrt(sums[0:1] * (1.0 / GROUP_WIDTH) + EPSILON)
+        slope = inv * inv * inv * sums[1:2] * (1.0 / GROUP_WIDTH)
+        rows[:, block] = jnp.where(iota((8, Q), 0) == 0, inv, slope)
+        return inv, slope
+
+    def scatter(parts, landing, block):
+        return [
+            remote(parts.at[pl.ds(k * W, W), block], landing.at[pl.ds(j * W, W), block], device)
+            for j, (k, device) in enumerate(((3, to_across), (2, to_right), (1, to_left)))
+        ]
+
+    c_sums = [scatter(c_part, recv_c, pl.ds(j * Q, Q)) for j in range(2)]
+    b_sums = scatter(b_part, recv_b, pl.ds(0, T))
+
+    def c_grad(j, block, until):
+        inv, slope = factors(j, block)
+        full = jnp.where(high[until, block], inv * d1[until, block] - slope * d2[until, block], 0.0)
+        th[until, block], tl[until, block] = halves(full)
+        grad = dot3((bh[:, until], bl[:, until]), (th[until, block], tl[until, block]))
+
+        @pl.when(early)
+        def _():
+            c_part[:, block] = grad
+
+        @pl.when(late)
+        def _():
+            c_part[:, block] = grad + (inv * k1[:, block] - slope * k2[:, block])
+
+        begin(c_sums[j])
+
+    c_grad(0, lo, lo)
+    c_grad(1, hi, slice(0, T))
+    th[hi, lo] = jnp.zeros((Q, Q), BF)
+    tl[hi, lo] = jnp.zeros((Q, Q), BF)
     rows_out = remote(rows, rows_in, to_core)
+    b_grad = dot3((ch[...], cl[...]), (th[...], tl[...]), NT)
 
     @pl.when(late)
     def _():
         rows_out.start()
-
-    full = jnp.where(high, inverse * d1[...] - slope * d2[...], 0.0)
-    th[...], tl[...] = halves(full)
-
-    def c_part():
-        return dot3((bh[...], bl[...]), (th[...], tl[...]))
-
-    def b_part():
-        return dot3((ch[...], cl[...]), (th[...], tl[...]), NT)
-
-    def scatter(parts, landing):
-        far = [
-            remote(parts.at[pl.ds(3 * W, half)], landing.at[pl.ds(0, half)], to_right),
-            remote(parts.at[pl.ds(3 * W + half, half)], landing.at[pl.ds(half, half)], to_left),
-        ]
-        near = [
-            remote(parts.at[pl.ds(2 * W + half, half)], landing.at[pl.ds(W + half, half)], to_right),
-            remote(parts.at[pl.ds(W, half)], landing.at[pl.ds(2 * W, half)], to_left),
-        ]
-        total = [
-            remote(parts.at[pl.ds(2 * W, half)], landing.at[pl.ds(W, half)], to_right),
-            remote(parts.at[pl.ds(W + half, half)], landing.at[pl.ds(2 * W + half, half)], to_left),
-        ]
-        return far, near, total
-
-    def relay(parts, landing, far, total):
-        far[0].wait_recv()
-        parts[2 * W:2 * W + half] += landing[0:half]
-        total[0].start()
-        far[1].wait_recv()
-        parts[W + half:2 * W] += landing[half:W]
-        total[1].start()
-
-    first_far, first_near, first_total = scatter(first, recv_a)
-    second_far, second_near, second_total = scatter(second, recv_b)
-
-    def begin(copies):
-        for copy in copies:
-            copy.start()
+        b_part[...] = b_grad
+        begin(b_sums)
 
     @pl.when(early)
     def _():
-        first[...] = c_part()
-        begin(first_far)
-        second[...] = b_part()
         aq_out.wait_recv()
         oh[...], ol[...] = halves(aq_in[...])
         k2[...] = dot3((wh[...], wl[...]), (oh[...], ol[...]), NT)
         rows_out.wait_recv()
         gth[...], gtl[...] = halves(rows_in[0:1] * k1[...] - rows_in[1:2] * k2[...])
-        second[...] += dot3((c1h[...], c1l[...]), (gth[...], gtl[...]), NT)
-        begin(second_far)
-
-    @pl.when(late)
-    def _():
-        first[...] = b_part()
-        begin(first_far)
-        second[...] = c_part() + (inverse * k1[...] - slope * k2[...])
-        begin(second_far)
-
-    begin(first_near)
+        b_part[...] = b_grad + dot3((c1h[...], c1l[...]), (gth[...], gtl[...]), NT)
+        begin(b_sums)
 
     lead = iota((128, T), 0)
-    cols[...] = jnp.where(lead == 0, inverse, jnp.where(lead == 1, slope, 0.0)).T
+    cols[...] = jnp.where(lead == 0, rows[0:1], jnp.where(lead == 1, rows[1:2], 0.0)).T
 
     def finish(r, carry):
         gain_sum, skip_sum = carry
@@ -462,12 +437,9 @@
     zero = jnp.zeros((8, D), F32)
     gain_sum, skip_sum = tiles(finish, init=(zero, zero))
 
-    begin(second_near)
-
     def turned(top, bottom):
         return (gh[top, bottom].astype(F32).T.astype(BF), gl[top, bottom].astype(F32).T.astype(BF))
 
-    lo, hi = slice(0, Q), slice(Q, T)
     g00, g10, g11 = turned(lo, lo), turned(hi, lo), turned(hi, hi)
     for k in range(2):
         part = pl.ds(k * 256, 256)
@@ -476,8 +448,6 @@
         ] * dot3(g10, (uh[Q:T, part], ul[Q:T, part]))
         dv[Q:T, part] = dot3(g11, (uh[Q:T, part], ul[Q:T, part]))
 
-    relay(first, recv_a, first_far, first_total)
-    relay(second, recv_b, second_far, second_total)
     small[0:16] = jnp.zeros((16, D), F32)
 
     def x_grad(r, f):
@@ -539,33 +509,25 @@
     small_out = remote(small.at[pl.ds(0, 8)], small.at[pl.ds(16, 8)], to_core)
     small_out.start()
 
-    for copy in small_out, *first_near, *first_total:
-        copy.wait_recv()
+    arrive([small_out] + c_sums[0] + c_sums[1])
     params[...] = small[0:8] + small[16:24]
-    first_sum = first[0:W] + (recv_a[W:2 * W] + recv_a[2 * W:3 * W])
-    for copy in second_near + second_total:
-        copy.wait_recv()
-    second_sum = second[0:W] + (recv_b[W:2 * W] + recv_b[2 * W:3 * W])
+    cgv[...] = c_part[0:W] + (recv_c[0:W] + (recv_c[W:2 * W] + recv_c[2 * W:3 * W]))
+    arrive(b_sums)
+    bgv[...] = b_part[0:W] + (recv_b[0:W] + (recv_b[W:2 * W] + recv_b[2 * W:3 * W]))
 
     @pl.when(early)
     def _():
-        cgv[...] = first_sum
-        bgv[...] = second_sum
         for copy in state_out:
             copy.wait_send()
 
     @pl.when(late)
     def _():
-        bgv[...] = first_sum
-        cgv[...] = second_sum
         for copy in (ap_out, aq_out, c_out, rows_out):
             copy.wait_send()
 
-    for copy in b_ahead + b_after + b_onward + c_ahead + c_after + c_onward + norm_out:
-        copy.wait_send()
-    for copy in first_far + first_near + first_total + second_far + second_near + second_total:
-        copy.wait_send()
-    small_out.wait_send()
+    for copies in (*b_copies, *c_copies, *norm_out, *c_sums, b_sums, [small_out]):
+        for copy in copies:
+            copy.wait_send()
 
 
 def place_results(*refs):
@@ -604,13 +566,13 @@
     scratch += [narrow] * 2 + [vb(Q, D)] * 2 + [narrow] * 10
     scratch += [thin] * 14 + [narrow] * 2 + [thin] * 2 + [narrow] * 2
     scratch += [vm(4, W, D)] * 2 + [narrow] * 2 + [wide] * 4 + [vm(8, T)] * 2
-    scratch += [wide] * 4 + [thin] * 2 + [vm(4, 8, T), vm(T, 128), vm(T, 128)]
+    scratch += [wide] * 4 + [thin] * 2 + [vm(2, 4, 8, Q), vm(T, 128), vm(T, 128)]
     scratch += [square] * 4 + [wide] + [narrow] * 2
     scratch += [wide] * 2 + [square] * 2 + [vm(3 * W, T)] * 2 + [vm(32, D)]
     scratch += [
         pltpu.SemaphoreType.DMA((10,)),
-        pltpu.SemaphoreType.DMA((37,)),
-        pltpu.SemaphoreType.DMA((37,)),
+        pltpu.SemaphoreType.DMA((36,)),
+        pltpu.SemaphoreType.DMA((36,)),
     ]
     args = [pltpu.with_memory_space_constraint(array, pltpu.HBM) for array in args]
     results = pl.pallas_call(

time: 33.3 us -> 32.6 us (0.979)
  Pallas kernels: 32.5 us -> 31.8 us
    pallas_call x1, Pallas kernels: 30.8 us -> 30.1 us  [shards(): pl.pallas_call(body, out_shape=[f32(T, D), f32(T, D), f32(T, D), f32(H, T...]
where the time goes in v5:
time: 32.6 us; the launch traced here: 32.5 us
  Pallas kernels  31.8 us (98%)
  between operations  0.65 us (2%)
    pallas_call x1, Pallas kernels, shards(): pl.pallas_call(body, out_shape=[f32(T, D), f32(T, D), f32(T, D), f32(H, T...  30.1 us
    pallas_call x1, Pallas kernels, shards(): pl.pallas_call(place_results, out_shape=[f32(T, D), f32(T, D), f32(T, D),...  1.76 us

profile of v5, /device:TPU:1, one launch (start us, length us, event | category | flops | bytes accessed | tf_op | source)
XLA Modules:
  0.0 32.5 jit_solution(3769712279752880015)
XLA Ops:
  0.6 30.1 %layer.1 = (f32[256,512]{1,0:T(8,128)S(1)}, f32[256,512]{1,0:T(8,128)S(1)}, f32[256,512]{1,0:T(8,128)S(1)}, f32[8,256]{1,0:T(8,128)S(1)}, f32[64,256]{1,0:T(8,12...) custom-call(f32[256,512]{1,0:T(8,128)} %x_in.1, f32[256,512]{1,0:T(8,128)} %z_in.1, f32[8,256]{1,0:T(8,128)} %raw_in.1, ...), custom_call_target="tpu_custom_call" | custom-call | tf_op jit(solution)/shard_map/layer/pallas_call | solution.py:578
  30.7 1.8 %place_results.1 = (f32[256,512]{1,0:T(8,128)}, f32[256,512]{1,0:T(8,128)}, f32[256,512]{1,0:T(8,128)}, f32[8,256]{1,0:T(8,128)}, f32[64,256]{1,0:T(8,128)}, /*i...) custom-call(f32[256,512]{1,0:T(8,128)S(1)} %get-tuple-element.17.refs_0_, ...), custom_call_target="tpu_custom_call" | custom-call | tf_op jit(solution)/shard_map/place_results/pallas_call | solution.py:589

commit v6 on v5

--- a/solution.py
+++ b/solution.py
@@ -74,7 +74,7 @@
     bh, bl, ch, cl, cth, ctl, bth, btl, c1h, c1l, gh, gl, gth, gtl, oh, ol, th, tl, fh, fl,
     state, other, sh, sl, ap, ap_in, aq, aq_in, rows, rows_in,
     yi, yv, gated, carry_v, sumh, suml, norm, cols, cols1, d1, d2, k1, k2, dy, yqh, yql,
-    dv, dx, b_part, c_part, recv_b, recv_c, small,
+    dv, dx, b_part, c_parts, recv_b, recv_c, small, crh, crl, turnh, turnl,
     local_sem, send_sem, recv_sem,
 ):
     dp = lax.axis_index("dp")
@@ -283,6 +283,19 @@
     def _():
         mix_early(0, lo)
 
+    def scatter(parts, landing):
+        return [
+            remote(parts.at[pl.ds(k * W, W)], landing.at[pl.ds(j * W, W)], device)
+            for j, (k, device) in enumerate(((3, to_across), (2, to_right), (1, to_left)))
+        ]
+
+    b_sums = scatter(b_part, recv_b)
+    c_sums = [scatter(c_parts.at[j], recv_c.at[j]) for j in range(2)]
+
+    def c_grad(j, grad):
+        th[...], tl[...] = halves(jnp.where(high, grad[...], 0.0))
+        return dot3((bh[...], bl[...]), (th[...], tl[...]))
+
     state_out = [remote(state.at[k], other.at[k], to_core) for k in range(4)]
     arrive(b_copies[1])
     bh[:, hi], bl[:, hi] = halves(bv[:, hi])
@@ -294,7 +307,13 @@
             state[k] = dot3((bh[part], bl[part]), (wh[...], wl[...]))
             state_out[k].start()
 
+    c_parts[0] = c_grad(0, d1)
     arrive(c_copies[1])
+
+    @pl.when(early)
+    def _():
+        begin(c_sums[0])
+
     cth[hi], ctl[hi] = halves(cv[:, hi].T)
     c_out = remote(cv, c1v, to_core)
 
@@ -340,23 +359,32 @@
         tiles(go, TILES // 2, first=Q)
         send_sums(1, hi)
         aq_out.start()
+        c_parts[0] += dot3((sh[...], sl[...]), (wh[...], wl[...]), NT)
+        begin(c_sums[0])
 
     score_grad(d2, qh, ql)
     ch[...], cl[...] = halves(cv[...])
 
     @pl.when(early)
     def _():
+        c_parts[1] = c_grad(1, d2)
+        begin(c_sums[1])
         ap_out.wait_recv()
         fh[...], fl[...] = halves(ap_in[...])
         k1[...] = dot3((wh[...], wl[...]), (fh[...], fl[...]), NT)
         bth[...], btl[...] = halves(bv[...].T)
         c_out.wait_recv()
         c1h[...], c1l[...] = halves(c1v[...])
+        crh[...], crl[...] = halves(dot3((bth[...], btl[...]), (c1h[...], c1l[...])))
 
     @pl.when(late)
     def _():
-        k1[...] = dot3((sh[...], sl[...]), (wh[...], wl[...]), NT)
-        k2[...] = dot3((sh[...], sl[...]), (eh[...], el[...]), NT)
+        c_parts[1] = c_grad(1, d2) + dot3((sh[...], sl[...]), (eh[...], el[...]), NT)
+        begin(c_sums[1])
+
+    for rows_of, cols_of in ((lo, lo), (hi, lo), (hi, hi)):
+        turnh[cols_of, rows_of] = gh[rows_of, cols_of].astype(F32).T.astype(BF)
+        turnl[cols_of, rows_of] = gl[rows_of, cols_of].astype(F32).T.astype(BF)
 
     def factors(j, block):
         arrive(norm_out[j])
@@ -364,37 +392,10 @@
         inv = lax.rsqrt(sums[0:1] * (1.0 / GROUP_WIDTH) + EPSILON)
         slope = inv * inv * inv * sums[1:2] * (1.0 / GROUP_WIDTH)
         rows[:, block] = jnp.where(iota((8, Q), 0) == 0, inv, slope)
-        return inv, slope
-
-    def scatter(parts, landing, block):
-        return [
-            remote(parts.at[pl.ds(k * W, W), block], landing.at[pl.ds(j * W, W), block], device)
-            for j, (k, device) in enumerate(((3, to_across), (2, to_right), (1, to_left)))
-        ]
-
-    c_sums = [scatter(c_part, recv_c, pl.ds(j * Q, Q)) for j in range(2)]
-    b_sums = scatter(b_part, recv_b, pl.ds(0, T))
-
-    def c_grad(j, block, until):
-        inv, slope = factors(j, block)
-        full = jnp.where(high[until, block], inv * d1[until, block] - slope * d2[until, block], 0.0)
-        th[until, block], tl[until, block] = halves(full)
-        grad = dot3((bh[:, until], bl[:, until]), (th[until, block], tl[until, block]))
-
-        @pl.when(early)
-        def _():
-            c_part[:, block] = grad
-
-        @pl.when(late)
-        def _():
-            c_part[:, block] = grad + (inv * k1[:, block] - slope * k2[:, block])
-
-        begin(c_sums[j])
-
-    c_grad(0, lo, lo)
-    c_grad(1, hi, slice(0, T))
-    th[hi, lo] = jnp.zeros((Q, Q), BF)
-    tl[hi, lo] = jnp.zeros((Q, Q), BF)
+
+    for j, block in enumerate((lo, hi)):
+        factors(j, block)
+    th[...], tl[...] = halves(jnp.where(high, rows[0:1] * d1[...] - rows[1:2] * d2[...], 0.0))
     rows_out = remote(rows, rows_in, to_core)
     b_grad = dot3((ch[...], cl[...]), (th[...], tl[...]), NT)
 
@@ -437,16 +438,12 @@
     zero = jnp.zeros((8, D), F32)
     gain_sum, skip_sum = tiles(finish, init=(zero, zero))
 
-    def turned(top, bottom):
-        return (gh[top, bottom].astype(F32).T.astype(BF), gl[top, bottom].astype(F32).T.astype(BF))
-
-    g00, g10, g11 = turned(lo, lo), turned(hi, lo), turned(hi, hi)
     for k in range(2):
         part = pl.ds(k * 256, 256)
-        dv[0:Q, part] = dot3(g00, (uh[0:Q, part], ul[0:Q, part])) + kappa[
+        dv[0:Q, part] = dot3((turnh[lo, lo], turnl[lo, lo]), (uh[0:Q, part], ul[0:Q, part])) + kappa[
             :, k * 256:(k + 1) * 256
-        ] * dot3(g10, (uh[Q:T, part], ul[Q:T, part]))
-        dv[Q:T, part] = dot3(g11, (uh[Q:T, part], ul[Q:T, part]))
+        ] * dot3((turnh[lo, hi], turnl[lo, hi]), (uh[Q:T, part], ul[Q:T, part]))
+        dv[Q:T, part] = dot3((turnh[hi, hi], turnl[hi, hi]), (uh[Q:T, part], ul[Q:T, part]))
 
     small[0:16] = jnp.zeros((16, D), F32)
 
@@ -463,10 +460,9 @@
             return carry
 
         tiles(later)
-        cross = halves(dot3((bth[...], btl[...]), (c1h[...], c1l[...])))
         for k in range(2):
             part = pl.ds(k * 256, 256)
-            dx[:, part] = dot3(cross, (eh[:, part], el[:, part]))
+            dx[:, part] = dot3((crh[...], crl[...]), (eh[:, part], el[:, part]))
 
         def go(r, carry):
             tail = a5[r] * dx[r]
@@ -511,7 +507,11 @@
 
     arrive([small_out] + c_sums[0] + c_sums[1])
     params[...] = small[0:8] + small[16:24]
-    cgv[...] = c_part[0:W] + (recv_c[0:W] + (recv_c[W:2 * W] + recv_c[2 * W:3 * W]))
+    c_total = [
+        c_parts[j, 0:W] + (recv_c[j, 0:W] + (recv_c[j, W:2 * W] + recv_c[j, 2 * W:3 * W]))
+        for j in range(2)
+    ]
+    cgv[...] = rows[0:1] * c_total[0] - rows[1:2] * c_total[1]
     arrive(b_sums)
     bgv[...] = b_part[0:W] + (recv_b[0:W] + (recv_b[W:2 * W] + recv_b[2 * W:3 * W]))
 
@@ -568,7 +568,7 @@
     scratch += [vm(4, W, D)] * 2 + [narrow] * 2 + [wide] * 4 + [vm(8, T)] * 2
     scratch += [wide] * 4 + [thin] * 2 + [vm(2, 4, 8, Q), vm(T, 128), vm(T, 128)]
     scratch += [square] * 4 + [wide] + [narrow] * 2
-    scratch += [wide] * 2 + [square] * 2 + [vm(3 * W, T)] * 2 + [vm(32, D)]
+    scratch += [wide] * 2 + [square, vm(2, N, T), vm(3 * W, T), vm(2, 3 * W, T), vm(32, D)] + [thin] * 4
     scratch += [
         pltpu.SemaphoreType.DMA((10,)),
         pltpu.SemaphoreType.DMA((36,)),

time: 32.6 us -> 32.5 us (level)
  no operation moved by 1% of the time
where the time goes in v6:
time: 32.5 us; the launch traced here: 32.3 us
  Pallas kernels  31.7 us (98%)
  between operations  0.65 us (2%)
    pallas_call x1, Pallas kernels, shards(): pl.pallas_call(body, out_shape=[f32(T, D), f32(T, D), f32(T, D), f32(H, T...  29.9 us
    pallas_call x1, Pallas kernels, shards(): pl.pallas_call(place_results, out_shape=[f32(T, D), f32(T, D), f32(T, D),...  1.76 us

profile of v6, /device:TPU:1, one launch (start us, length us, event | category | flops | bytes accessed | tf_op | source)
XLA Modules:
  0.0 32.3 jit_solution(898031734566836787)
XLA Ops:
  0.6 29.9 %layer.1 = (f32[256,512]{1,0:T(8,128)S(1)}, f32[256,512]{1,0:T(8,128)S(1)}, f32[256,512]{1,0:T(8,128)S(1)}, f32[8,256]{1,0:T(8,128)S(1)}, f32[64,256]{1,0:T(8,12...) custom-call(f32[256,512]{1,0:T(8,128)} %x_in.1, f32[256,512]{1,0:T(8,128)} %z_in.1, f32[8,256]{1,0:T(8,128)} %raw_in.1, ...), custom_call_target="tpu_custom_call" | custom-call | tf_op jit(solution)/shard_map/layer/pallas_call | solution.py:578
  30.6 1.8 %place_results.1 = (f32[256,512]{1,0:T(8,128)}, f32[256,512]{1,0:T(8,128)}, f32[256,512]{1,0:T(8,128)}, f32[8,256]{1,0:T(8,128)}, f32[64,256]{1,0:T(8,128)}, /*i...) custom-call(f32[256,512]{1,0:T(8,128)S(1)} %get-tuple-element.17.refs_0_, ...), custom_call_target="tpu_custom_call" | custom-call | tf_op jit(solution)/shard_map/place_results/pallas_call | solution.py:589

commit v7 on v6

--- a/solution.py
+++ b/solution.py
@@ -58,7 +58,7 @@
     def run(i, carry):
         return step(pl.ds(pl.multiple_of(first + i * ROWS, ROWS), ROWS), carry)
 
-    return lax.fori_loop(0, count, run, 0 if init is None else init)
+    return lax.fori_loop(0, count, run, 0 if init is None else init, unroll=True)
 
 
 def iota(shape, dim):
@@ -376,6 +376,9 @@
         c_out.wait_recv()
         c1h[...], c1l[...] = halves(c1v[...])
         crh[...], crl[...] = halves(dot3((bth[...], btl[...]), (c1h[...], c1l[...])))
+        aq_out.wait_recv()
+        oh[...], ol[...] = halves(aq_in[...])
+        k2[...] = dot3((wh[...], wl[...]), (oh[...], ol[...]), NT)
 
     @pl.when(late)
     def _():
@@ -407,9 +410,6 @@
 
     @pl.when(early)
     def _():
-        aq_out.wait_recv()
-        oh[...], ol[...] = halves(aq_in[...])
-        k2[...] = dot3((wh[...], wl[...]), (oh[...], ol[...]), NT)
         rows_out.wait_recv()
         gth[...], gtl[...] = halves(rows_in[0:1] * k1[...] - rows_in[1:2] * k2[...])
         b_part[...] = b_grad + dot3((c1h[...], c1l[...]), (gth[...], gtl[...]), NT)

time: 32.5 us -> 30.4 us (0.935)
  Pallas kernels: 31.7 us -> 29.6 us
    pallas_call x1, Pallas kernels: 29.9 us -> 27.8 us  [shards(): pl.pallas_call(body, out_shape=[f32(T, D), f32(T, D), f32(T, D), f32(H, T...]
where the time goes in v7:
time: 30.4 us; the launch traced here: 30.3 us
  Pallas kernels  29.6 us (97%)
  between operations  0.65 us (2%)
    pallas_call x1, Pallas kernels, shards(): pl.pallas_call(body, out_shape=[f32(T, D), f32(T, D), f32(T, D), f32(H, T...  27.8 us
    pallas_call x1, Pallas kernels, shards(): pl.pallas_call(place_results, out_shape=[f32(T, D), f32(T, D), f32(T, D),...  1.76 us

profile of v7, /device:TPU:1, one launch (start us, length us, event | category | flops | bytes accessed | tf_op | source)
XLA Modules:
  0.0 30.3 jit_solution(8999926794908235755)
XLA Ops:
  0.6 27.8 %layer.1 = (f32[256,512]{1,0:T(8,128)S(1)}, f32[256,512]{1,0:T(8,128)S(1)}, f32[256,512]{1,0:T(8,128)S(1)}, f32[8,256]{1,0:T(8,128)S(1)}, f32[64,256]{1,0:T(8,12...) custom-call(f32[256,512]{1,0:T(8,128)} %x_in.1, f32[256,512]{1,0:T(8,128)} %z_in.1, f32[8,256]{1,0:T(8,128)} %raw_in.1, ...), custom_call_target="tpu_custom_call" | custom-call | tf_op jit(solution)/shard_map/layer/pallas_call | solution.py:578
  28.5 1.8 %place_results.1 = (f32[256,512]{1,0:T(8,128)}, f32[256,512]{1,0:T(8,128)}, f32[256,512]{1,0:T(8,128)}, f32[8,256]{1,0:T(8,128)}, f32[64,256]{1,0:T(8,128)}, /*i...) custom-call(f32[256,512]{1,0:T(8,128)S(1)} %get-tuple-element.17.refs_0_, ...), custom_call_target="tpu_custom_call" | custom-call | tf_op jit(solution)/shard_map/place_results/pallas_call | solution.py:589

commit v8 on v7

--- a/solution.py
+++ b/solution.py
@@ -73,8 +73,8 @@
     vh, vl, kh, kl, wh, wl, ph, pld, qh, ql, eh, el, uh, ul,
     bh, bl, ch, cl, cth, ctl, bth, btl, c1h, c1l, gh, gl, gth, gtl, oh, ol, th, tl, fh, fl,
     state, other, sh, sl, ap, ap_in, aq, aq_in, rows, rows_in,
-    yi, yv, gated, carry_v, sumh, suml, norm, cols, cols1, d1, d2, k1, k2, dy, yqh, yql,
-    dv, dx, b_part, c_parts, recv_b, recv_c, small, crh, crl, turnh, turnl,
+    yi, yv, gated, carry_v, sumh, suml, norm, cols, d1, d2, k1, k2, dy, yqh, yql,
+    dv, dx, b_part, c_parts, recv_b, recv_c, small, crs, turnh, turnl,
     local_sem, send_sem, recv_sem,
 ):
     dp = lax.axis_index("dp")
@@ -162,7 +162,7 @@
 
     b_copies = [gather(b_in, bv, j) for j in range(2)]
     c_copies = [gather(c_in, cv, j) for j in range(2)]
-    begin(b_copies[0] + c_copies[0])
+    begin(b_copies[0] + b_copies[1])
 
     total0 = run[:, Q - 1:Q]
     total1 = run[:, T - 1:T]
@@ -182,7 +182,7 @@
     for k, ref in enumerate((a1, a2, a5)):
         spread = jnp.where(same & (row // 32 == k), 1.0, 0.0).astype(BF)
         ref[...] = dot(stacked, spread)
-    begin(b_copies[1] + c_copies[1])
+    begin(c_copies[0] + c_copies[1])
 
     own = iota((H, D), 0) == iota((H, D), 1) // W
     kappa = jnp.sum(
@@ -237,8 +237,18 @@
     high = src <= dst
     get_b.wait()
     get_c.wait()
-    arrive(b_copies[0])
-    bh[:, lo], bl[:, lo] = halves(bv[:, lo])
+    arrive(b_copies[0] + b_copies[1])
+    bh[...], bl[...] = halves(bv[...])
+
+    state_out = [remote(state.at[k], other.at[k], to_core) for k in range(4)]
+
+    @pl.when(early)
+    def _():
+        for k in range(4):
+            part = slice(k * W, (k + 1) * W)
+            state[k] = dot3((bh[part], bl[part]), (wh[...], wl[...]))
+            state_out[k].start()
+
     arrive(c_copies[0])
     cth[lo], ctl[lo] = halves(cv[:, lo].T)
     g0 = dot3((cth[lo], ctl[lo]), (bh[:, lo], bl[:, lo]))
@@ -295,17 +305,6 @@
     def c_grad(j, grad):
         th[...], tl[...] = halves(jnp.where(high, grad[...], 0.0))
         return dot3((bh[...], bl[...]), (th[...], tl[...]))
-
-    state_out = [remote(state.at[k], other.at[k], to_core) for k in range(4)]
-    arrive(b_copies[1])
-    bh[:, hi], bl[:, hi] = halves(bv[:, hi])
-
-    @pl.when(early)
-    def _():
-        for k in range(4):
-            part = slice(k * W, (k + 1) * W)
-            state[k] = dot3((bh[part], bl[part]), (wh[...], wl[...]))
-            state_out[k].start()
 
     c_parts[0] = c_grad(0, d1)
     arrive(c_copies[1])
@@ -375,7 +374,7 @@
         bth[...], btl[...] = halves(bv[...].T)
         c_out.wait_recv()
         c1h[...], c1l[...] = halves(c1v[...])
-        crh[...], crl[...] = halves(dot3((bth[...], btl[...]), (c1h[...], c1l[...])))
+        crs[...] = dot3((bth[...], btl[...]), (c1h[...], c1l[...]))
         aq_out.wait_recv()
         oh[...], ol[...] = halves(aq_in[...])
         k2[...] = dot3((wh[...], wl[...]), (oh[...], ol[...]), NT)
@@ -385,6 +384,19 @@
         c_parts[1] = c_grad(1, d2) + dot3((sh[...], sl[...]), (eh[...], el[...]), NT)
         begin(c_sums[1])
 
+    heads = jnp.where(own, 1.0, 0.0).astype(BF)
+
+    def weigh(r, carry):
+        gy = gate[r] * yv[r]
+        uh[r], ul[r] = halves(ogg[r] * gy)
+        yqh[r], yql[r] = halves(gated[r] * gy)
+        return carry
+
+    tiles(weigh)
+    y_sums = [
+        dot(heads, high_part[...], NT) + dot(heads, low_part[...], NT)
+        for high_part, low_part in ((uh, ul), (yqh, yql))
+    ]
     for rows_of, cols_of in ((lo, lo), (hi, lo), (hi, hi)):
         turnh[cols_of, rows_of] = gh[rows_of, cols_of].astype(F32).T.astype(BF)
         turnl[cols_of, rows_of] = gl[rows_of, cols_of].astype(F32).T.astype(BF)
@@ -432,7 +444,6 @@
         d = grad * gate[r]
         dy[r] = d
         uh[r], ul[r] = halves(a1[r] * d)
-        yqh[r], yql[r] = halves(d * y)
         return gain_sum + fold(ogv[r] * normed), skip_sum + fold(d * x)
 
     zero = jnp.zeros((8, D), F32)
@@ -453,16 +464,17 @@
 
     @pl.when(early)
     def _():
-        cols1[...] = jnp.where(lead == 0, rows_in[0:1], jnp.where(lead == 1, rows_in[1:2], 0.0)).T
-
-        def later(r, carry):
-            eh[r], el[r] = halves(cols1[r, 0:1] * ap_in[r] - cols1[r, 1:2] * aq_in[r])
-            return carry
-
-        tiles(later)
+        scaled = [halves(crs[...] * rows_in[0:1]), halves(crs[...] * -rows_in[1:2])]
+        cross = [jnp.concatenate([scaled[0][k], scaled[1][k]], axis=1) for k in range(2)]
         for k in range(2):
             part = pl.ds(k * 256, 256)
-            dx[:, part] = dot3((crh[...], crl[...]), (eh[:, part], el[:, part]))
+            dx[:, part] = dot3(
+                cross,
+                (
+                    jnp.concatenate([fh[:, part], oh[:, part]], axis=0),
+                    jnp.concatenate([fl[:, part], ol[:, part]], axis=0),
+                ),
+            )
 
         def go(r, carry):
             tail = a5[r] * dx[r]
@@ -480,8 +492,7 @@
         tiles(go)
 
 
-    heads = jnp.where(own, 1.0, 0.0).astype(BF)
-    y_sum = dot(heads, yqh[...], NT) + dot(heads, yql[...], NT)
+    y_sum = rows[0:1] * y_sums[0] - rows[1:2] * y_sums[1]
     x_sum = dot(heads, uh[...], NT) + dot(heads, ul[...], NT)
     from_end = jnp.sum(
         jnp.where(own, jnp.sum(small[8:16], axis=0, keepdims=True), 0.0), axis=1, keepdims=True
@@ -566,9 +577,9 @@
     scratch += [narrow] * 2 + [vb(Q, D)] * 2 + [narrow] * 10
     scratch += [thin] * 14 + [narrow] * 2 + [thin] * 2 + [narrow] * 2
     scratch += [vm(4, W, D)] * 2 + [narrow] * 2 + [wide] * 4 + [vm(8, T)] * 2
-    scratch += [wide] * 4 + [thin] * 2 + [vm(2, 4, 8, Q), vm(T, 128), vm(T, 128)]
+    scratch += [wide] * 4 + [thin] * 2 + [vm(2, 4, 8, Q), vm(T, 128)]
     scratch += [square] * 4 + [wide] + [narrow] * 2
-    scratch += [wide] * 2 + [square, vm(2, N, T), vm(3 * W, T), vm(2, 3 * W, T), vm(32, D)] + [thin] * 4
+    scratch += [wide] * 2 + [square, vm(2, N, T), vm(3 * W, T), vm(2, 3 * W, T), vm(32, D), square] + [thin] * 2
     scratch += [
         pltpu.SemaphoreType.DMA((10,)),
         pltpu.SemaphoreType.DMA((36,)),

time: 30.4 us -> 30 us (0.987)
  Pallas kernels: 29.6 us -> 29.2 us
    pallas_call x1, Pallas kernels: 27.8 us -> 27.5 us  [shards(): pl.pallas_call(body, out_shape=[f32(T, D), f32(T, D), f32(T, D), f32(H, T...]
where the time goes in v8:
time: 30 us; the launch traced here: 29.9 us
  Pallas kernels  29.2 us (97%)
  between operations  0.65 us (2%)
    pallas_call x1, Pallas kernels, shards(): pl.pallas_call(body, out_shape=[f32(T, D), f32(T, D), f32(T, D), f32(H, T...  27.5 us
    pallas_call x1, Pallas kernels, shards(): pl.pallas_call(place_results, out_shape=[f32(T, D), f32(T, D), f32(T, D),...  1.76 us

profile of v8, /device:TPU:1, one launch (start us, length us, event | category | flops | bytes accessed | tf_op | source)
XLA Modules:
  0.0 29.9 jit_solution(17837312747762227700)
XLA Ops:
  0.6 27.5 %layer.1 = (f32[256,512]{1,0:T(8,128)S(1)}, f32[256,512]{1,0:T(8,128)S(1)}, f32[256,512]{1,0:T(8,128)S(1)}, f32[8,256]{1,0:T(8,128)S(1)}, f32[64,256]{1,0:T(8,12...) custom-call(f32[256,512]{1,0:T(8,128)} %x_in.1, f32[256,512]{1,0:T(8,128)} %z_in.1, f32[8,256]{1,0:T(8,128)} %raw_in.1, ...), custom_call_target="tpu_custom_call" | custom-call | tf_op jit(solution)/shard_map/layer/pallas_call | solution.py:589
  28.1 1.8 %place_results.1 = (f32[256,512]{1,0:T(8,128)}, f32[256,512]{1,0:T(8,128)}, f32[256,512]{1,0:T(8,128)}, f32[8,256]{1,0:T(8,128)}, f32[64,256]{1,0:T(8,128)}, /*i...) custom-call(f32[256,512]{1,0:T(8,128)S(1)} %get-tuple-element.17.refs_0_, ...), custom_call_target="tpu_custom_call" | custom-call | tf_op jit(solution)/shard_map/place_results/pallas_call | solution.py:600

commit v9 on v8

--- a/solution.py
+++ b/solution.py
@@ -362,7 +362,6 @@
         begin(c_sums[0])
 
     score_grad(d2, qh, ql)
-    ch[...], cl[...] = halves(cv[...])
 
     @pl.when(early)
     def _():
@@ -384,6 +383,7 @@
         c_parts[1] = c_grad(1, d2) + dot3((sh[...], sl[...]), (eh[...], el[...]), NT)
         begin(c_sums[1])
 
+    ch[...], cl[...] = halves(cv[...])
     heads = jnp.where(own, 1.0, 0.0).astype(BF)
 
     def weigh(r, carry):
@@ -410,13 +410,17 @@
 
     for j, block in enumerate((lo, hi)):
         factors(j, block)
+    rows_out = remote(rows, rows_in, to_core)
+
+    @pl.when(late)
+    def _():
+        rows_out.start()
+
     th[...], tl[...] = halves(jnp.where(high, rows[0:1] * d1[...] - rows[1:2] * d2[...], 0.0))
-    rows_out = remote(rows, rows_in, to_core)
     b_grad = dot3((ch[...], cl[...]), (th[...], tl[...]), NT)
 
     @pl.when(late)
     def _():
-        rows_out.start()
         b_part[...] = b_grad
         begin(b_sums)
 

time: 30 us -> 30 us (level)
  no operation moved by 1% of the time
where the time goes in v9:
time: 30 us; the launch traced here: 29.9 us
  Pallas kernels  29.2 us (97%)
  between operations  0.65 us (2%)
    pallas_call x1, Pallas kernels, shards(): pl.pallas_call(body, out_shape=[f32(T, D), f32(T, D), f32(T, D), f32(H, T...  27.5 us
    pallas_call x1, Pallas kernels, shards(): pl.pallas_call(place_results, out_shape=[f32(T, D), f32(T, D), f32(T, D),...  1.76 us

profile of v9, /device:TPU:1, one launch (start us, length us, event | category | flops | bytes accessed | tf_op | source)
XLA Modules:
  0.0 29.9 jit_solution(4756138191862052865)
XLA Ops:
  0.6 27.5 %layer.1 = (f32[256,512]{1,0:T(8,128)S(1)}, f32[256,512]{1,0:T(8,128)S(1)}, f32[256,512]{1,0:T(8,128)S(1)}, f32[8,256]{1,0:T(8,128)S(1)}, f32[64,256]{1,0:T(8,12...) custom-call(f32[256,512]{1,0:T(8,128)} %x_in.1, f32[256,512]{1,0:T(8,128)} %z_in.1, f32[8,256]{1,0:T(8,128)} %raw_in.1, ...), custom_call_target="tpu_custom_call" | custom-call | tf_op jit(solution)/shard_map/layer/pallas_call | solution.py:593
  28.1 1.8 %place_results.1 = (f32[256,512]{1,0:T(8,128)}, f32[256,512]{1,0:T(8,128)}, f32[256,512]{1,0:T(8,128)}, f32[8,256]{1,0:T(8,128)}, f32[64,256]{1,0:T(8,128)}, /*i...) custom-call(f32[256,512]{1,0:T(8,128)S(1)} %get-tuple-element.17.refs_0_, ...), custom_call_target="tpu_custom_call" | custom-call | tf_op jit(solution)/shard_map/place_results/pallas_call | solution.py:604
